TPU v7x, 32 devices: a whole 2x2x4 slice. The times are simulated.
32 devices in a mesh: rows: 4 (over y, x), tp: 8 (over z, core).
Axes of the slice: x: 2, y: 2, z: 4, core: 2. Of those that a mesh axis runs over, the one named last changes fastest.
Arguments:
- block_input: bfloat16 [4096, 2048], P(('rows', 'tp')), may hold values from -6 to 6
- norm_gain: bfloat16 [2048], replicated, may hold values from 0.5 to 1.5
- norm_bias: bfloat16 [2048], replicated, may hold values from -1.5 to 1.5
- qkv_weight: bfloat16 [3, 2048, 2048], P(None, 'tp'), may hold values from -0.125 to 0.125
- qkv_bias: bfloat16 [3, 2048], P(None, 'tp'), may hold values from -1 to 1
- out_weight: bfloat16 [2048, 2048], P('tp'), may hold values from -0.75 to 0.75
- gate_weight: bfloat16 [5632, 2048], P('tp'), may hold values from -0.125 to 0.125
- up_weight: bfloat16 [5632, 2048], P('tp'), may hold values from -0.125 to 0.125
- down_weight: bfloat16 [5632, 2048], P('tp'), may hold values from -0.078125 to 0.078125
- cotangent: bfloat16 [4096, 2048], P(('rows', 'tp')), may hold values from -6 to 6
- doc_lengths: int32 [4, 8], P('rows'), may hold values from 1 to 512, 1024 in all within a row
Outputs:
- output: bfloat16 [4096, 2048], P(('rows', 'tp'))
- input_grad: float32 [4096, 2048], P(('rows', 'tp'))
- gain_grad: float32 [2048], replicated
- bias_grad: float32 [2048], replicated
- qkv_grad: float32 [3, 2048, 2048], P(None, 'tp')
- qkv_bias_grad: float32 [3, 2048], P(None, 'tp')
- out_grad: float32 [2048, 2048], P('tp')
- gate_grad: float32 [5632, 2048], P('tp')
- up_grad: float32 [5632, 2048], P('tp')
- down_grad: float32 [5632, 2048], P('tp')
Inputs may be any that keep to these rules, and one draw needn't show every extreme that they name: `doc_lengths`: each row holds the lengths of the 8 consecutive pieces of one packed row in order, summing to 1024; the last piece is padding; in every row the longest piece has exactly 512 tokens.
All inputs are finite; a program needn't handle non-finite values.
Results may differ from a plain program's by a relative error of at most 0.0099.
Values may be sent and summed in bfloat16 or wider, within the bound.
No kernel may reach another device: no remote copies, remote signals or barrier semaphores. Data moves between devices by JAX's collectives and lax.ppermute only.
A program may use at most 192 MiB of HBM per device.

v0:
```python
import jax
import jax.numpy as jnp
from jax import lax
from jax.sharding import PartitionSpec as P

HEAD = 64
ROT = 16
DOCS = 8


EPSILON = 1e-05
MASKED = -1e30


def layout(doc_lengths, row_len):
    ends = jnp.cumsum(doc_lengths, axis=1)
    starts = ends - doc_lengths
    places = jnp.arange(row_len, dtype=jnp.int32)
    segment = jnp.sum((places[None, :, None] >= ends[:, None, :]).astype(jnp.int32), axis=2)
    chosen = segment[:, :, None] == jnp.arange(DOCS, dtype=jnp.int32)[None, None, :]
    first = jnp.sum(jnp.where(chosen, starts[:, None, :], 0), axis=2)
    position = places[None, :] - first
    live = segment < DOCS - 1
    return (segment, position, live)


def angles(position):
    half = ROT // 2
    freq = 10000.0 ** (-(jnp.arange(half).astype(jnp.float32) * (2.0 / ROT)))
    angle = position.astype(jnp.float32)[..., None] * freq
    return (jnp.cos(angle)[..., None, :], jnp.sin(angle)[..., None, :])


def rotate(values, position):
    half = ROT // 2
    cosine, sine = angles(position)
    first = values[..., :half]
    second = values[..., half:ROT]
    return jnp.concatenate(
        [first * cosine - second * sine, second * cosine + first * sine, values[..., ROT:]], axis=-1
    )


def unrotate(grads, position):
    half = ROT // 2
    cosine, sine = angles(position)
    first = grads[..., :half]
    second = grads[..., half:ROT]
    return jnp.concatenate(
        [first * cosine + second * sine, second * cosine - first * sine, grads[..., ROT:]], axis=-1
    )


def standardize(values):
    centre = jnp.mean(values, axis=1, keepdims=True)
    centred = values - centre
    spread = jnp.mean(centred * centred, axis=1, keepdims=True)
    inverse = lax.rsqrt(spread + EPSILON)
    return (centred * inverse, inverse)


def project(hidden_in, qkv_weight, qkv_bias, gate_weight, up_weight, position):
    packs = position.shape[0]
    row_len = position.shape[1]
    heads = qkv_weight.shape[1] // HEAD
    lines = jnp.einsum("td,jed->jte", hidden_in, qkv_weight, preferred_element_type=jnp.float32)
    lines = lines + qkv_bias.astype(jnp.float32)[:, None, :]
    shape = (packs, row_len, heads, HEAD)
    query = rotate(lines[0].reshape(shape), position).astype(jnp.bfloat16)
    key = rotate(lines[1].reshape(shape), position).astype(jnp.bfloat16)
    value = lines[2].reshape(shape).astype(jnp.bfloat16)
    gate = jnp.einsum("td,fd->tf", hidden_in, gate_weight, preferred_element_type=jnp.float32)
    up = jnp.einsum("td,fd->tf", hidden_in, up_weight, preferred_element_type=jnp.float32)
    return (query, key, value, gate, up)


def block_allowed(segment, start, size):
    places = jnp.arange(segment.shape[0], dtype=jnp.int32)
    rows_here = start + jnp.arange(size, dtype=jnp.int32)
    segment_rows = lax.dynamic_slice_in_dim(segment, start, size)
    return (segment_rows[:, None] == segment[None, :]) & (places[None, :] <= rows_here[:, None])


def attend_forward(query, key, value, segment):
    length = query.shape[0]
    size = min(512, length)
    scale = HEAD ** (-0.5)

    def one_block(index):
        start = index * size
        block = lax.dynamic_slice_in_dim(query, start, size)
        scores = jnp.einsum("qhd,khd->hqk", block, key, preferred_element_type=jnp.float32) * scale
        scores = jnp.where(block_allowed(segment, start, size)[None], scores, MASKED)
        highest = jnp.max(scores, axis=2, keepdims=True)
        raised = jnp.exp(scores - highest)
        total = jnp.sum(raised, axis=2, keepdims=True)
        weights = (raised / total).astype(jnp.bfloat16)
        context = jnp.einsum("hqk,khd->qhd", weights, value, preferred_element_type=jnp.float32)
        return (context.astype(jnp.bfloat16), (highest + jnp.log(total))[:, :, 0])

    context, logsum = lax.map(one_block, jnp.arange(length // size, dtype=jnp.int32))
    return (context.reshape(length, -1), logsum)


def attend_backward(query, key, value, segment, context_grad, logsum):
    length = query.shape[0]
    size = min(512, length)
    scale = HEAD ** (-0.5)

    def one_block(carry, index):
        key_grad, value_grad = carry
        start = index * size
        block = lax.dynamic_slice_in_dim(query, start, size)
        block_grad = lax.dynamic_slice_in_dim(context_grad, start, size)
        scores = jnp.einsum("qhd,khd->hqk", block, key, preferred_element_type=jnp.float32) * scale
        allowed = block_allowed(segment, start, size)[None]
        probs = jnp.where(allowed, jnp.exp(scores - logsum[index][:, :, None]), 0.0)
        value_grad = value_grad + jnp.einsum(
            "hqk,qhd->khd",
            probs.astype(jnp.bfloat16),
            block_grad,
            preferred_element_type=jnp.float32,
        )
        prob_grad = jnp.einsum(
            "qhd,khd->hqk", block_grad, value, preferred_element_type=jnp.float32
        )
        inner = jnp.sum(probs * prob_grad, axis=2, keepdims=True)
        score_low = (probs * (prob_grad - inner)).astype(jnp.bfloat16)
        query_grad = (
            jnp.einsum("hqk,khd->qhd", score_low, key, preferred_element_type=jnp.float32) * scale
        )
        key_grad = (
            key_grad
            + jnp.einsum("hqk,qhd->khd", score_low, block, preferred_element_type=jnp.float32)
            * scale
        )
        return ((key_grad, value_grad), query_grad)

    zeros = jnp.zeros(key.shape, jnp.float32)
    (key_grad, value_grad), query_grad = lax.scan(
        one_block, (zeros, zeros), jnp.arange(length // size, dtype=jnp.int32)
    )
    return (query_grad.reshape(key.shape), key_grad, value_grad)


def per_device(
    block_input,
    norm_gain,
    norm_bias,
    qkv_weight,
    qkv_bias,
    out_weight,
    gate_weight,
    up_weight,
    down_weight,
    cotangent,
    doc_lengths,
):
    shard = block_input.shape[0]
    tokens = shard * lax.axis_size("tp")
    width = qkv_weight.shape[1]
    heads = width // HEAD
    packs = doc_lengths.shape[0]
    row_len = tokens // packs
    segment, position, live = layout(doc_lengths, row_len)
    live_all = live.reshape(tokens)
    live_mine = lax.dynamic_slice_in_dim(live_all, lax.axis_index("tp") * shard, shard).astype(
        jnp.float32
    )
    input_wide = block_input.astype(jnp.float32)
    gain = norm_gain.astype(jnp.float32)
    shift = norm_bias.astype(jnp.float32)
    normed, inverse = standardize(input_wide)
    normed_low = (normed * gain + shift).astype(jnp.bfloat16)
    hidden_in = lax.all_gather(normed_low, "tp", axis=0, tiled=True)
    query, key, value, gate, up = project(
        hidden_in, qkv_weight, qkv_bias, gate_weight, up_weight, position
    )
    mixed = (jax.nn.silu(gate) * up).astype(jnp.bfloat16)
    pack = 0
    context_part, logsum = attend_forward(query[pack], key[pack], value[pack], segment[pack])
    logsums = [logsum]
    part_mixed = mixed
    merged = lax.psum_scatter(
        jnp.dot(context_part, out_weight, preferred_element_type=jnp.float32)
        + jnp.dot(part_mixed, down_weight, preferred_element_type=jnp.float32),
        "tp",
        scatter_dimension=0,
        tiled=True,
    )
    output = (input_wide + live_mine[:, None] * merged).astype(jnp.bfloat16)
    normed, inverse = standardize(input_wide)
    normed_low = (normed * gain + shift).astype(jnp.bfloat16)
    hidden_in, grad_all = (
        lax.all_gather(normed_low, "tp", axis=0, tiled=True),
        lax.all_gather(cotangent, "tp", axis=0, tiled=True),
    )
    query, key, value, gate, up = project(
        hidden_in, qkv_weight, qkv_bias, gate_weight, up_weight, position
    )
    mixed = (jax.nn.silu(gate) * up).astype(jnp.bfloat16)
    grad_low = grad_all * live_all.astype(jnp.bfloat16)[:, None]
    context_grad = jnp.dot(grad_low, out_weight.T, preferred_element_type=jnp.float32).astype(
        jnp.bfloat16
    )
    mixed_grad = jnp.dot(grad_low, down_weight.T, preferred_element_type=jnp.float32)
    out_grad = jnp.dot(context_part.T, grad_low, preferred_element_type=jnp.float32)
    down_grad = jnp.dot(mixed.T, grad_low, preferred_element_type=jnp.float32)
    sigmoid = jax.nn.sigmoid(gate)
    gate_low = (mixed_grad * up * sigmoid * (1.0 + gate * (1.0 - sigmoid))).astype(jnp.bfloat16)
    up_low = (mixed_grad * gate * sigmoid).astype(jnp.bfloat16)
    gate_grad = jnp.einsum("tf,td->fd", gate_low, hidden_in, preferred_element_type=jnp.float32)
    up_grad = jnp.einsum("tf,td->fd", up_low, hidden_in, preferred_element_type=jnp.float32)
    context_grad = context_grad.reshape(packs, row_len, heads, HEAD)
    pack = 0
    query_part, key_part, value_part = attend_backward(
        query[pack], key[pack], value[pack], segment[pack], context_grad[pack], logsums[pack]
    )
    query_parts = [query_part]
    key_parts = [key_part]
    value_parts = [value_part]
    query_grad = unrotate(jnp.stack(query_parts), position).reshape(tokens, width)
    key_grad = unrotate(jnp.stack(key_parts), position).reshape(tokens, width)
    value_grad = jnp.stack(value_parts).reshape(tokens, width)
    lines_low = jnp.stack([query_grad, key_grad, value_grad]).astype(jnp.bfloat16)
    qkv_grad = jnp.einsum("jte,td->jed", lines_low, hidden_in, preferred_element_type=jnp.float32)
    qkv_bias_grad = jnp.sum(lines_low, axis=1, dtype=jnp.float32)
    term = jnp.einsum("jte,jed->td", lines_low, qkv_weight, preferred_element_type=jnp.float32)
    term = term + jnp.dot(gate_low, gate_weight, preferred_element_type=jnp.float32)
    normed_grad = lax.psum_scatter(
        term + jnp.dot(up_low, up_weight, preferred_element_type=jnp.float32),
        "tp",
        scatter_dimension=0,
        tiled=True,
    )
    scaled = normed_grad * gain
    input_grad = inverse * (
        scaled
        - jnp.mean(scaled, axis=1, keepdims=True)
        - normed * jnp.mean(scaled * normed, axis=1, keepdims=True)
    )
    input_grad = input_grad + cotangent.astype(jnp.float32)
    gain_grad, bias_grad = lax.psum(
        (jnp.sum(normed_grad * normed, axis=0), jnp.sum(normed_grad, axis=0)), ("rows", "tp")
    )
    qkv_grad, qkv_bias_grad, out_grad, gate_grad, up_grad, down_grad = lax.psum(
        (qkv_grad, qkv_bias_grad, out_grad, gate_grad, up_grad, down_grad), "rows"
    )
    return (
        output,
        input_grad,
        gain_grad,
        bias_grad,
        qkv_grad,
        qkv_bias_grad,
        out_grad,
        gate_grad,
        up_grad,
        down_grad,
    )


def solution(mesh):
    placed = (
        P(("rows", "tp"), None),
        P(),
        P(),
        P(None, "tp", None),
        P(None, "tp"),
        P("tp", None),
        P("tp", None),
        P("tp", None),
        P("tp", None),
        P(("rows", "tp"), None),
        P("rows", None),
    )
    return jax.shard_map(
        per_device,
        mesh=mesh,
        in_specs=placed,
        out_specs=(
            P(("rows", "tp"), None),
            P(("rows", "tp"), None),
            P(),
            P(),
            P(None, "tp", None),
            P(None, "tp"),
            P("tp", None),
            P("tp", None),
            P("tp", None),
            P("tp", None),
        ),
        check_vma=False,
    )
```

profile of v0, /device:TPU:0, one launch (start us, length us, event | category | flops | bytes accessed | tf_op | source)
XLA Modules:
  0.0 921.6 jit_solution(15409836116185560561)
XLA Ops:
  17.7 46.6 %all-gather.3.cloned.1.call-done = bf16[1024,2048]{1,0:T(8,128)(2,1)} async-done(((bf16[128,2048]{1,0:T(8,128)(2,1)}), bf16[1024,2048]{1,0:T(8,128)(2,1)}) %all-gather.3.cloned.1.call-update) | async-done | bytes 4194320 | tf_op jit(solution)/shard_map/all_gather | solution.py:175
  64.3 5.3 add_bitcast_fusion
  71.9 21.9 %while.27 = (s32[]{:T(128)}, bf16[2,512,4,64]{1,3,2,0:T(8,128)(2,1)}, f32[2,4,512]{2,1,0:T(4,128)S(1)}, s32[2]{0:T(128)S(1)}, s32[1024]{0:T(1024)S(1)}, /*index=...) while((s32[]{:T(128)}, ...), condition=%wide.region_8.9_spmd, body=%wide.region_5.8_spmd.sunk | while | flops 563739136 | bytes 35207460 | solution.py:101
  73.8 2.8 fusion.141
  76.7 2.3 fusion.142
  79.0 3.0 fusion.143
  84.8 2.8 fusion.141
  87.6 2.3 fusion.142
  90.0 3.0 fusion.143
  93.8 18.0 %all-gather.5.cloned.1.call-done = bf16[1024,2048]{1,0:T(8,128)(2,1)} async-done(((bf16[128,2048]{1,0:T(8,128)(2,1)}), bf16[1024,2048]{1,0:T(8,128)(2,1)}) %all-gather.5.cloned.1.call-update) | async-done | bytes 4194320 | tf_op jit(solution)/shard_map/all_gather | solution.py:196
  111.8 4.6 fusion.57
  116.4 86.1 %while.28 = (s32[]{:T(128)}, f32[1024,4,64]{0,2,1:T(8,128)}, f32[1024,4,64]{0,2,1:T(8,128)}, f32[2,512,4,64]{1,0,3,2:T(2,128)}, s32[2]{0:T(128)S(1)}, /*index=5*...) while((s32[]{:T(128)}, f32[1024,4,64]{0,2,1:T(8,128)}, ...), condition=%wide.region_12.13_spmd.clone, body=%wide.region_10.12_spmd.clone.sunk | while | flops 1376647680 | bytes 133241392 | solution.py:140
  117.8 5.7 fusion.153
  126.2 7.0 multiply_reduce_fusion.3
  133.2 3.7 multiply_convert_fusion.5
  137.0 4.2 fusion.155
  141.2 5.0 fusion.156
  149.0 10.4 %dynamic_update_slice.20 = f32[2,512,4,64]{1,0,3,2:T(2,128)} dynamic-update-slice(f32[2,512,4,64]{1,0,3,2:T(2,128)} %get-tuple-element.441, f32[1,512,4,64]{1,0,3,2:T(1,128)} %copy.49, s32[]{:T(128)S(6)} %copy.66, s32[]{:T(128)} %constant.46.clone.1..sunk.1, s32[]{:T(128)} %constant.46.clone.1..sunk.1, s32[]{:T(128)} %constant.46.clone.1..sunk.1) | dynamic-update-slice | bytes 1048580 | tf_op jit(solution)/shard_map/while/body/jit(dynamic_update_index_in_dim)/dynamic_update_slice | solution.py:140
  160.7 5.7 fusion.153
  169.0 7.0 multiply_reduce_fusion.3
  176.1 3.7 multiply_convert_fusion.5
  179.8 4.5 fusion.155
  184.4 5.0 fusion.156
  192.1 10.4 %dynamic_update_slice.20 = f32[2,512,4,64]{1,0,3,2:T(2,128)} dynamic-update-slice(f32[2,512,4,64]{1,0,3,2:T(2,128)} %get-tuple-element.441, f32[1,512,4,64]{1,0,3,2:T(1,128)} %copy.49, s32[]{:T(128)S(6)} %copy.66, s32[]{:T(128)} %constant.46.clone.1..sunk.1, s32[]{:T(128)} %constant.46.clone.1..sunk.1, s32[]{:T(128)} %constant.46.clone.1..sunk.1) | dynamic-update-slice | bytes 1048580 | tf_op jit(solution)/shard_map/while/body/jit(dynamic_update_index_in_dim)/dynamic_update_slice | solution.py:140
  203.7 3.1 stack_reshape.11
  210.7 6.7 fusion.47
  217.4 3.2 fusion.83
  220.6 5.5 multiply_convert_fusion.2
  226.1 5.6 fusion.86
  231.7 5.7 fusion.85
  248.0 10.0 %fusion.38 = f32[1024,2048]{1,0:T(8,128)} fusion(f32[1024,2048]{1,0:T(8,128)} %fusion.86, f32[1024,2048]{1,0:T(8,128)} %fusion.85, bf16[3,256,2048]{2,1,0:T(8,128)(2,1)S(1)} %copy-done, bf16[1,1024,256]{2,1,0:T(8,128)(2,1)} %copy.35, bf16[1,1024,256]{2,1,0:T(8,128)(2,1)} %copy.34, bf16[1,1024,256]{2,1,0:T(8,128)(2,1)} %copy.33), kind=kOutput, calls=%fused_computation.48 | convolution fusion | flops 3226992640 | bytes 29884416 | tf_op jit(solution)/shard_map/jte,jed->td/dot_general | solution.py:228
  260.1 5.9 fusion.84
  266.1 4.6 convolution_add_fusion
  270.8 5.2 fusion.45
  275.9 5.0 fusion.87
  280.9 4.9 fusion.88
  285.8 5.1 fusion.43
  290.9 5.4 fusion.39
  298.0 10.6 %psum.59 = f32[3,256]{1,0:T(4,128)} all-reduce(f32[3,256]{1,0:T(4,128)S(1)} %convert_reduce_fusion), channel_id=1, replica_groups=mesh['rows'=4,'tp'=8] {'rows'}, use_global_device_ids=true, to_apply=%region_22.23 | all-reduce | flops 768 | bytes 6144 | tf_op jit(solution)/shard_map/psum | solution.py:246
  308.6 37.9 %reduce-scatter.5.cloned.1.call-done = f32[128,2048]{1,0:T(8,128)} async-done(((f32[1024,2048]{1,0:T(8,128)}), f32[128,2048]{1,0:T(8,128)}) %reduce-scatter.5.cloned.1.call-update) | async-done | bytes 1048592 | tf_op jit(solution)/shard_map/reduce_scatter | solution.py:230
  348.3 39.7 %all-reduce = (f32[2048]{0:T(1024)}, f32[2048]{0:T(1024)}) all-reduce(f32[2048]{0:T(1024)S(1)} %get-tuple-element.166, f32[2048]{0:T(1024)S(1)} %get-tuple-element.169), channel_id=1, replica_groups=mesh['rows'=4,'tp'=8] {'rows','tp'}, use_global_device_ids=true, to_apply=%region_17.18 | all-reduce | flops 4096 | bytes 32768 | tf_op jit(solution)/shard_map/psum | solution.py:243
  388.0 49.7 %reduce-scatter.3.cloned.1.call-done = f32[128,2048]{1,0:T(8,128)} async-done(((f32[1024,2048]{1,0:T(8,128)}), f32[128,2048]{1,0:T(8,128)}) %reduce-scatter.3.cloned.1.call-update) | async-done | bytes 1048592 | tf_op jit(solution)/shard_map/reduce_scatter | solution.py:184
  437.7 3.5 fusion.71
  441.2 455.6 %all-reduce.4.cloned.1.call-done = (f32[3,256,2048]{2,1,0:T(8,128)}, f32[256,2048]{1,0:T(8,128)}, f32[704,2048]{1,0:T(8,128)}, f32[704,2048]{1,0:T(8,128)}, f32[704,2048]{1,0:T(8,128)}) async-done(((f32[3,256,2048]{2,1,0:T(8,128)}, f32[256,2048]{1,0:T(8,128)}, f32[704,2048]{1,0:T(8,128)}, f32[704,2048]{1,0:T(8,128)}, f32[704,2048]{1,0:T(8,128)}), (f32[3,256,2048]{2,1,0:T(8,128)}, f32[256,2048]{1,0:T(8,128)}, ...) | async-done | bytes 25690128 | tf_op jit(solution)/shard_map/psum | solution.py:246
  896.8 6.9 copy.79
  905.0 2.9 copy.81
  908.0 2.9 copy.82
  912.3 2.5 copy.83
  (194 shorter events, 48.8 us)
Async XLA Ops:
  7.2 57.1 %copy-start = (bf16[3,256,2048]{2,1,0:T(8,128)(2,1)S(1)}, bf16[3,256,2048]{2,1,0:T(8,128)(2,1)}, u32[]{:S(2)}) copy-start(bf16[3,256,2048]{2,1,0:T(8,128)(2,1)} %param.18) | copy-start | bytes 9437188
  7.2 57.1 %all-gather.3.cloned.1.call-start = ((), (), s32[]{:S(2)}) async-start(), calls=%async_computation.2 | async-start | bytes 4718592 | tf_op jit(solution)/shard_map/all_gather | solution.py:175
  14.3 97.5 %all-gather.5.cloned.1.call-start = ((), (), s32[]{:S(2)}) async-start(), calls=%async_computation.4 | async-start | bytes 4718592 | tf_op jit(solution)/shard_map/all_gather | solution.py:196
  15.0 331.5 %reduce-scatter.5.cloned.1.call-start = ((), (), s32[]{:S(2)}) async-start(), calls=%async_computation.5 | async-start | bytes 9437184 | tf_op jit(solution)/shard_map/reduce_scatter | solution.py:230
  17.7 52.9 %copy-start.21 = (f32[1024,8]{0,1:T(8,128)}, f32[1024,8]{0,1:T(8,128)S(1)}, u32[]{:S(2)}) copy-start(f32[1024,8]{0,1:T(8,128)S(1)} %get-tuple-element.242) | copy-start | bytes 98308
  17.7 52.9 %copy-start.22 = (f32[1024,8]{0,1:T(8,128)}, f32[1024,8]{0,1:T(8,128)S(1)}, u32[]{:S(2)}) copy-start(f32[1024,8]{0,1:T(8,128)S(1)} %get-tuple-element.243) | copy-start | bytes 98308
  126.1 7.1 copy-start.3
  126.1 7.1 slice-start
  126.2 7.1 slice-start.1
  136.9 4.2 copy-start.4
  137.0 4.2 copy-start.13
  137.0 4.2 copy-start.16
  141.2 5.1 copy-start.1
  141.2 5.0 copy-start.2
  169.0 7.1 copy-start.3
  169.0 7.1 slice-start
  169.0 7.1 slice-start.1
  179.8 4.5 copy-start.4
  179.8 4.5 copy-start.13
  179.8 4.5 copy-start.16
  184.3 5.1 copy-start.1
  184.3 5.1 copy-start.2
  210.7 6.7 copy-start.10
  210.7 6.7 copy-start.30
  226.1 5.6 copy-start.33
  226.1 5.6 copy-start.35
  231.7 5.7 copy-start.18
  258.0 179.7 %reduce-scatter.3.cloned.1.call-start = ((), (), s32[]{:S(2)}) async-start(), calls=%async_computation.3 | async-start | bytes 9437184 | tf_op jit(solution)/shard_map/reduce_scatter | solution.py:184
  260.1 6.0 copy-start.12
  260.1 6.0 copy-start.15
  270.7 626.1 %all-reduce.4.cloned.1.call-start = ((), (), s32[]{:S(2)}) async-start(), calls=%async_computation.6 | async-start | bytes 51380224 | tf_op jit(solution)/shard_map/psum | solution.py:246
  270.7 5.2 copy-start.11
  270.7 5.2 copy-start.36
  275.9 5.0 copy-start.34
  280.9 5.0 copy-start.29
  280.9 5.0 copy-start.32
  285.8 5.1 copy-start.6
  285.8 5.1 copy-start.7
  285.8 5.1 copy-start.8
  296.3 50.2 %copy-start.24 = (f32[2048]{0:T(1024)S(1)}, f32[2048]{0:T(1024)}, u32[]{:S(2)}) copy-start(f32[2048]{0:T(1024)} %copy-done.23) | copy-start | bytes 24580
  296.3 50.2 %copy-start.26 = (f32[128]{0:T(128)S(1)}, f32[128]{0:T(128)}, u32[]{:S(2)}) copy-start(f32[128]{0:T(128)} %copy-done.25) | copy-start | bytes 1540
  296.3 50.2 %copy-start.28 = (f32[128]{0:T(128)S(1)}, f32[128]{0:T(128)}, u32[]{:S(2)}) copy-start(f32[128]{0:T(128)} %copy-done.27) | copy-start | bytes 1540
  896.8 6.9 copy-start.14
  896.8 8.3 copy-start.9
  896.8 11.2 %slice-start.4 = ((s8[5767168]{0:T(1024)(128)(4,1)}), s8[4194304]{0:T(1024)(128)(4,1)S(1)}, s32[]{:S(2)}) async-start(s8[5767168]{0:T(1024)(128)(4,1)} %bitcast.142), calls=%async_computation.11 | async-start | bytes 8388608
  903.7 4.3 slice-start.5
  905.0 7.1 slice-start.2
  908.0 4.3 slice-start.3
  (12 other events, 21.6 us)
Sparse Core Ops, SparseCore 0:
  14.4 49.8 all-gather.2
  65.9 45.8 all-gather.4
  258.1 88.3 reduce-scatter.4
  348.6 89.0 reduce-scatter.2
  443.0 453.7 all-reduce.3
where the time goes:
time: 930 us; the launch traced here: 922 us
  waiting for transfers between devices  608 us (65%)
  matrix products  141 us (15%)
  local copies, waits for them, and re-layouts  61.7 us (7%)
  blocking collectives  50.3 us (5%)
  other arithmetic  37.8 us (4%)
  between operations  14.3 us (2%)
    psum x1, waiting for transfers between devices, per_device(): lax.psum((qkv_grad, qkv_bias_grad, out_grad, gate_grad, up_grad, down_gra...  456 us
    reduce_scatter x1, waiting for transfers between devices, per_device(): lax.psum_scatter(jnp.dot(context_part, out_weight, preferred_element_type...  49.7 us
    all_gather x1, waiting for transfers between devices, per_device(): hidden_in = lax.all_gather(normed_low, 'tp', axis=0, tiled=True)  46.6 us
    psum x1, blocking collectives, per_device(): lax.psum((jnp.sum(normed_grad * normed, axis=0), jnp.sum(normed_grad, axi...  39.7 us
    reduce_scatter x1, waiting for transfers between devices, per_device(): lax.psum_scatter(term + jnp.dot(up_low, up_weight, preferred_element_type...  37.9 us
    dynamic_update_slice x4, local copies, waits for them, and re-layouts, attend_backward(): lax.scan(one_block, (zeros, zeros), jnp.arange(length // size, dtype=jnp....  23.5 us
    unnamed x68, local copies, waits for them, and re-layouts  18.8 us
  transfers between devices with their start and end apart: 5, of which 5 were waited for; matrix products, arithmetic and copies ran while one was open for 8% of the time, Pallas kernels for 0%

commit v1 on v0

--- a/solution.py
+++ b/solution.py
@@ -141,6 +141,13 @@
         one_block, (zeros, zeros), jnp.arange(length // size, dtype=jnp.int32)
     )
     return (query_grad.reshape(key.shape), key_grad, value_grad)
+
+
+def over_rows(partial, earlier=None):
+    partial = partial.astype(jnp.bfloat16)
+    if earlier is not None:
+        partial, _ = lax.optimization_barrier((partial, earlier))
+    return lax.psum(partial, "rows")
 
 
 def per_device(
@@ -178,61 +185,58 @@
     )
     mixed = (jax.nn.silu(gate) * up).astype(jnp.bfloat16)
     pack = 0
+    grad_all = lax.all_gather(cotangent, "tp", axis=0, tiled=True)
+    grad_low = grad_all * live_all.astype(jnp.bfloat16)[:, None]
+    down_sum = over_rows(jnp.dot(mixed.T, grad_low, preferred_element_type=jnp.float32))
     context_part, logsum = attend_forward(query[pack], key[pack], value[pack], segment[pack])
-    logsums = [logsum]
-    part_mixed = mixed
+    out_sum = over_rows(
+        jnp.dot(context_part.T, grad_low, preferred_element_type=jnp.float32), down_sum
+    )
     merged = lax.psum_scatter(
-        jnp.dot(context_part, out_weight, preferred_element_type=jnp.float32)
-        + jnp.dot(part_mixed, down_weight, preferred_element_type=jnp.float32),
+        (
+            jnp.dot(context_part, out_weight, preferred_element_type=jnp.float32)
+            + jnp.dot(mixed, down_weight, preferred_element_type=jnp.float32)
+        ).astype(jnp.bfloat16),
         "tp",
         scatter_dimension=0,
         tiled=True,
-    )
+    ).astype(jnp.float32)
     output = (input_wide + live_mine[:, None] * merged).astype(jnp.bfloat16)
-    normed, inverse = standardize(input_wide)
-    normed_low = (normed * gain + shift).astype(jnp.bfloat16)
-    hidden_in, grad_all = (
-        lax.all_gather(normed_low, "tp", axis=0, tiled=True),
-        lax.all_gather(cotangent, "tp", axis=0, tiled=True),
-    )
-    query, key, value, gate, up = project(
-        hidden_in, qkv_weight, qkv_bias, gate_weight, up_weight, position
-    )
-    mixed = (jax.nn.silu(gate) * up).astype(jnp.bfloat16)
-    grad_low = grad_all * live_all.astype(jnp.bfloat16)[:, None]
-    context_grad = jnp.dot(grad_low, out_weight.T, preferred_element_type=jnp.float32).astype(
-        jnp.bfloat16
-    )
     mixed_grad = jnp.dot(grad_low, down_weight.T, preferred_element_type=jnp.float32)
-    out_grad = jnp.dot(context_part.T, grad_low, preferred_element_type=jnp.float32)
-    down_grad = jnp.dot(mixed.T, grad_low, preferred_element_type=jnp.float32)
     sigmoid = jax.nn.sigmoid(gate)
     gate_low = (mixed_grad * up * sigmoid * (1.0 + gate * (1.0 - sigmoid))).astype(jnp.bfloat16)
     up_low = (mixed_grad * gate * sigmoid).astype(jnp.bfloat16)
-    gate_grad = jnp.einsum("tf,td->fd", gate_low, hidden_in, preferred_element_type=jnp.float32)
-    up_grad = jnp.einsum("tf,td->fd", up_low, hidden_in, preferred_element_type=jnp.float32)
+    gate_sum = over_rows(
+        jnp.einsum("tf,td->fd", gate_low, hidden_in, preferred_element_type=jnp.float32), out_sum
+    )
+    up_sum = over_rows(
+        jnp.einsum("tf,td->fd", up_low, hidden_in, preferred_element_type=jnp.float32), gate_sum
+    )
+    context_grad = jnp.dot(grad_low, out_weight.T, preferred_element_type=jnp.float32).astype(
+        jnp.bfloat16
+    )
     context_grad = context_grad.reshape(packs, row_len, heads, HEAD)
-    pack = 0
     query_part, key_part, value_part = attend_backward(
-        query[pack], key[pack], value[pack], segment[pack], context_grad[pack], logsums[pack]
-    )
-    query_parts = [query_part]
-    key_parts = [key_part]
-    value_parts = [value_part]
-    query_grad = unrotate(jnp.stack(query_parts), position).reshape(tokens, width)
-    key_grad = unrotate(jnp.stack(key_parts), position).reshape(tokens, width)
-    value_grad = jnp.stack(value_parts).reshape(tokens, width)
+        query[pack], key[pack], value[pack], segment[pack], context_grad[pack], logsum
+    )
+    query_grad = unrotate(query_part[None], position).reshape(tokens, width)
+    key_grad = unrotate(key_part[None], position).reshape(tokens, width)
+    value_grad = value_part.reshape(tokens, width)
     lines_low = jnp.stack([query_grad, key_grad, value_grad]).astype(jnp.bfloat16)
-    qkv_grad = jnp.einsum("jte,td->jed", lines_low, hidden_in, preferred_element_type=jnp.float32)
-    qkv_bias_grad = jnp.sum(lines_low, axis=1, dtype=jnp.float32)
+    qkv_sum = over_rows(
+        jnp.einsum("jte,td->jed", lines_low, hidden_in, preferred_element_type=jnp.float32), up_sum
+    )
+    qkv_bias_grad = lax.psum(jnp.sum(lines_low, axis=1, dtype=jnp.float32), "rows")
     term = jnp.einsum("jte,jed->td", lines_low, qkv_weight, preferred_element_type=jnp.float32)
     term = term + jnp.dot(gate_low, gate_weight, preferred_element_type=jnp.float32)
     normed_grad = lax.psum_scatter(
-        term + jnp.dot(up_low, up_weight, preferred_element_type=jnp.float32),
+        (term + jnp.dot(up_low, up_weight, preferred_element_type=jnp.float32)).astype(
+            jnp.bfloat16
+        ),
         "tp",
         scatter_dimension=0,
         tiled=True,
-    )
+    ).astype(jnp.float32)
     scaled = normed_grad * gain
     input_grad = inverse * (
         scaled
@@ -243,20 +247,17 @@
     gain_grad, bias_grad = lax.psum(
         (jnp.sum(normed_grad * normed, axis=0), jnp.sum(normed_grad, axis=0)), ("rows", "tp")
     )
-    qkv_grad, qkv_bias_grad, out_grad, gate_grad, up_grad, down_grad = lax.psum(
-        (qkv_grad, qkv_bias_grad, out_grad, gate_grad, up_grad, down_grad), "rows"
-    )
     return (
         output,
         input_grad,
         gain_grad,
         bias_grad,
-        qkv_grad,
+        qkv_sum.astype(jnp.float32),
         qkv_bias_grad,
-        out_grad,
-        gate_grad,
-        up_grad,
-        down_grad,
+        out_sum.astype(jnp.float32),
+        gate_sum.astype(jnp.float32),
+        up_sum.astype(jnp.float32),
+        down_sum.astype(jnp.float32),
     )
 
 

time: 930 us -> 675 us (0.73)
  waiting for transfers between devices: 608 us -> 339 us
  other arithmetic: 37.8 us -> 58.3 us
  local copies, waits for them, and re-layouts: 61.7 us -> 48.8 us
    psum x1 -> x5, waiting for transfers between devices: 456 us -> 216 us  [over_rows(): return lax.psum(partial, 'rows')]
    reduce_scatter x2, waiting for transfers between devices: 87.6 us -> 42.4 us  [the longest x1 31.7 us: per_device(): lax.psum_scatter((term + jnp.dot(up_low, up_weight, preferred_element_typ...]
    convert_element_type x0 -> x5, other arithmetic: none -> 18.9 us  [the longest x1 5.44 us: per_device(): qkv_sum.astype(jnp.float32)]
    all_gather x1, waiting for transfers between devices: 18 us -> 34 us  [per_device(): grad_all = lax.all_gather(cotangent, 'tp', axis=0, tiled=True)]
    unnamed x68 -> x61, local copies, waits for them, and re-layouts: 18.8 us -> 3.46 us
  transfers between devices with their start and end apart: 5 -> 9, of which waited for: 5 -> 8; matrix products, arithmetic and copies ran while one was open for 8% -> 33% of each run, Pallas kernels for 0% -> 0%
where the time goes in v1:
time: 675 us; the launch traced here: 665 us
  waiting for transfers between devices  339 us (50%)
  matrix products  146 us (22%)
  other arithmetic  58.3 us (9%)
  blocking collectives  49.3 us (7%)
  local copies, waits for them, and re-layouts  48.8 us (7%)
  between operations  14.7 us (2%)
  loops' own time  7.06 us (1%)
    psum x5, waiting for transfers between devices, over_rows(): return lax.psum(partial, 'rows')  216 us
    all_gather x1, waiting for transfers between devices, per_device(): hidden_in = lax.all_gather(normed_low, 'tp', axis=0, tiled=True)  45.9 us
    psum x1, blocking collectives, per_device(): lax.psum((jnp.sum(normed_grad * normed, axis=0), jnp.sum(normed_grad, axi...  39.7 us
    all_gather x1, waiting for transfers between devices, per_device(): grad_all = lax.all_gather(cotangent, 'tp', axis=0, tiled=True)  34 us
    reduce_scatter x1, waiting for transfers between devices, per_device(): lax.psum_scatter((term + jnp.dot(up_low, up_weight, preferred_element_typ...  31.7 us
    dynamic_update_slice x4, local copies, waits for them, and re-layouts, attend_backward(): lax.scan(one_block, (zeros, zeros), jnp.arange(length // size, dtype=jnp....  23.5 us
    dot_general x4, matrix products, one_block(): jnp.einsum('qhd,khd->hqk', block, key, preferred_element_type=jnp.float32)  17 us
    dot_general x2, matrix products, one_block(): jnp.einsum('qhd,khd->hqk', block_grad, value, preferred_element_type=jnp....  14 us
  transfers between devices with their start and end apart: 9, of which 8 were waited for; matrix products, arithmetic and copies ran while one was open for 33% of the time, Pallas kernels for 0%

profile of v1, /device:TPU:0, one launch (start us, length us, event | category | flops | bytes accessed | tf_op | source)
XLA Modules:
  0.0 664.5 jit_solution(16287223687263164725)
XLA Ops:
  17.7 45.9 %all-gather.3.cloned.1.call-done = bf16[1024,2048]{1,0:T(8,128)(2,1)} async-done(((bf16[128,2048]{1,0:T(8,128)(2,1)}), bf16[1024,2048]{1,0:T(8,128)(2,1)}) %all-gather.3.cloned.1.call-update) | async-done | bytes 4194320 | tf_op jit(solution)/shard_map/all_gather | solution.py:182
  63.6 5.4 add_bitcast_fusion
  72.4 4.8 fusion.90
  77.1 34.0 %all-gather.5.cloned.1.call-done = bf16[1024,2048]{1,0:T(8,128)(2,1)} async-done(((bf16[128,2048]{1,0:T(8,128)(2,1)}), bf16[1024,2048]{1,0:T(8,128)(2,1)}) %all-gather.5.cloned.1.call-update) | async-done | bytes 4194320 | tf_op jit(solution)/shard_map/all_gather | solution.py:188
  111.1 6.5 fusion.50
  117.6 5.7 multiply_convert_fusion.2
  124.5 4.6 convolution_convert_fusion
  132.9 21.4 %while.27 = (s32[]{:T(128)}, bf16[2,512,4,64]{1,3,2,0:T(8,128)(2,1)}, f32[2,4,512]{2,1,0:T(4,128)}, s32[2]{0:T(128)S(1)}, s32[1024]{0:T(1024)S(1)}, /*index=5*/s...) while((s32[]{:T(128)}, ...), condition=%wide.region_8.9_spmd, body=%wide.region_5.8_spmd.sunk | while | flops 563739136 | bytes 31144732 | solution.py:101
  134.8 2.8 fusion.146
  140.0 3.6 fusion.148
  145.5 2.8 fusion.146
  150.7 3.6 fusion.148
  156.8 5.0 fusion.54
  161.7 49.0 %all-reduce.7.cloned.1.call-done = bf16[704,2048]{1,0:T(8,128)(2,1)} async-done(((bf16[704,2048]{1,0:T(8,128)(2,1)}), bf16[704,2048]{1,0:T(8,128)(2,1)}) %all-reduce.7.cloned.1.call-update) | async-done | bytes 2883600 | tf_op jit(solution)/shard_map/psum | solution.py:150
  210.8 4.8 fusion.66
  215.7 4.5 convolution_convert_fusion.1
  220.1 46.4 %all-reduce.9.cloned.1.call-done = bf16[256,2048]{1,0:T(8,128)(2,1)} async-done(((bf16[256,2048]{1,0:T(8,128)(2,1)}), bf16[256,2048]{1,0:T(8,128)(2,1)}) %all-reduce.9.cloned.1.call-update) | async-done | bytes 1048592 | tf_op jit(solution)/shard_map/psum | solution.py:150
  266.8 90.6 %while.28 = (s32[]{:T(128)}, f32[1024,4,64]{0,2,1:T(8,128)}, f32[1024,4,64]{0,2,1:T(8,128)}, f32[2,512,4,64]{1,0,3,2:T(2,128)}, s32[2]{0:T(128)S(1)}, /*index=5*...) while((s32[]{:T(128)}, f32[1024,4,64]{0,2,1:T(8,128)}, ...), condition=%wide.region_12.13_spmd.clone, body=%wide.region_10.12_spmd.clone.sunk | while | flops 1376647680 | bytes 124852720 | solution.py:140
  269.6 5.6 fusion.158
  277.2 7.0 %multiply_reduce_fusion.2 = (f32[4,512]{1,0:T(4,128)S(1)}, f32[4,512,1024]{2,1,0:T(8,128)S(1)}) fusion(f32[4,512,1024]{2,1,0:T(8,128)} %fusion.158, f32[4,512]{1,0:T(4,128)S(1)} %dynamic-slice_bitcast_fusion.2, pred[512,1024]{1,0:T(8,128)(4,1)} %fusion.159, bf16[1024,4,64]{0,2,1:T(8,128)(2,1)} %get-tuple-element.469, ...), kind=kOutput, calls=%fused_computation.19.clone.1 | convolution fusion | flops 278919168 | bytes 18104324 | tf_op jit(solution)/shard_map/while/body/eval_jaxpr/qhd,khd->hqk/dot_general | solution.py:124
  284.3 2.4 multiply_convert_fusion.5
  291.4 10.4 %dynamic_update_slice.20 = f32[2,512,4,64]{1,0,3,2:T(2,128)} dynamic-update-slice(f32[2,512,4,64]{1,0,3,2:T(2,128)} %get-tuple-element.444, f32[1,512,4,64]{1,0,3,2:T(1,128)} %copy.49, s32[]{:T(128)} %get-tuple-element.441, s32[]{:T(128)} %constant.46.clone.1..sunk.1, s32[]{:T(128)} %constant.46.clone.1..sunk.1, s32[]{:T(128)} %constant.46.clone.1..sunk.1) | dynamic-update-slice | bytes 1048580 | tf_op jit(solution)/shard_map/while/body/jit(dynamic_update_index_in_dim)/dynamic_update_slice | solution.py:140
  301.8 4.2 fusion.160
  306.0 5.7 fusion.161
  314.4 5.8 fusion.158
  322.2 7.0 %multiply_reduce_fusion.2 = (f32[4,512]{1,0:T(4,128)S(1)}, f32[4,512,1024]{2,1,0:T(8,128)S(1)}) fusion(f32[4,512,1024]{2,1,0:T(8,128)} %fusion.158, f32[4,512]{1,0:T(4,128)S(1)} %dynamic-slice_bitcast_fusion.2, pred[512,1024]{1,0:T(8,128)(4,1)} %fusion.159, bf16[1024,4,64]{0,2,1:T(8,128)(2,1)} %get-tuple-element.469, ...), kind=kOutput, calls=%fused_computation.19.clone.1 | convolution fusion | flops 278919168 | bytes 18104324 | tf_op jit(solution)/shard_map/while/body/eval_jaxpr/qhd,khd->hqk/dot_general | solution.py:124
  336.4 10.4 %dynamic_update_slice.20 = f32[2,512,4,64]{1,0,3,2:T(2,128)} dynamic-update-slice(f32[2,512,4,64]{1,0,3,2:T(2,128)} %get-tuple-element.444, f32[1,512,4,64]{1,0,3,2:T(1,128)} %copy.49, s32[]{:T(128)} %get-tuple-element.441, s32[]{:T(128)} %constant.46.clone.1..sunk.1, s32[]{:T(128)} %constant.46.clone.1..sunk.1, s32[]{:T(128)} %constant.46.clone.1..sunk.1) | dynamic-update-slice | bytes 1048580 | tf_op jit(solution)/shard_map/while/body/jit(dynamic_update_index_in_dim)/dynamic_update_slice | solution.py:140
  346.8 4.5 fusion.160
  351.3 6.0 fusion.161
  357.5 3.1 broadcast_in_dim_reshape.3
  367.7 7.4 %convolution_convert_fusion.2 = bf16[704,2048]{1,0:T(8,128)(2,1)} fusion(bf16[1024,704]{0,1:T(8,128)(2,1)} %get-tuple-element.228, bf16[1024,2048]{1,0:T(8,128)(2,1)} %all-gather.3.cloned.1.call-done), kind=kOutput, calls=%fused_computation.58 | convolution fusion | flops 2954231808 | bytes 8519680 | tf_op jit(solution)/shard_map/tf,td->fd/dot_general | solution.py:213
  383.1 5.9 fusion.92
  389.1 5.8 fusion.93
  394.9 7.6 %fusion.39 = bf16[1024,2048]{1,0:T(8,128)(2,1)} fusion(f32[1024,2048]{1,0:T(8,128)} %fusion.93, f32[1024,2048]{1,0:T(8,128)S(1)} %fusion.92, bf16[3,256,2048]{2,1,0:T(8,128)(2,1)S(1)} %copy-done, bf16[1,1024,256]{2,1,0:T(8,128)(2,1)S(1)} %copy-done.15, bf16[1,1024,256]{2,1,0:T(8,128)(2,1)S(1)} %copy-done.14, bf16[1,1024,256]{2,1,0:T(8,128)(2,1)S(1)} %copy-done.13), kind=kOutput, calls=%fused_computation.49 | convolution fusion | flops 3229089792 | bytes 25690112 | tf_op jit(solution)/shard_map/jte,jed->td/dot_general | solution.py:230
  402.9 5.9 fusion.91
  408.8 3.3 add_convert_fusion
  412.2 7.9 %fusion.44 = bf16[3,256,2048]{2,1,0:T(8,128)(2,1)} fusion(bf16[1024,2048]{1,0:T(8,128)(2,1)} %all-gather.3.cloned.1.call-done, bf16[1,1024,256]{2,1,0:T(8,128)(2,1)} %copy.35, bf16[1,1024,256]{2,1,0:T(8,128)(2,1)} %copy.34, bf16[1,1024,256]{2,1,0:T(8,128)(2,1)} %copy.33), kind=kOutput, calls=%fused_computation.55 | convolution fusion | flops 3224371200 | bytes 8912896 | tf_op jit(solution)/shard_map/jte,td->jed/dot_general | solution.py:227
  420.1 38.0 %all-reduce.13.cloned.1.call-done = bf16[704,2048]{1,0:T(8,128)(2,1)} async-done(((bf16[704,2048]{1,0:T(8,128)(2,1)}), bf16[704,2048]{1,0:T(8,128)(2,1)}) %all-reduce.13.cloned.1.call-update) | async-done | bytes 2883600 | tf_op jit(solution)/shard_map/psum | solution.py:150
  459.8 9.5 %psum.63 = f32[3,256]{1,0:T(4,128)} all-reduce(f32[3,256]{1,0:T(4,128)S(1)} %convert_reduce_fusion), channel_id=1, replica_groups=mesh['rows'=4,'tp'=8] {'rows'}, use_global_device_ids=true, to_apply=%region_26.27 | all-reduce | flops 768 | bytes 6144 | tf_op jit(solution)/shard_map/psum | solution.py:229
  469.3 5.3 convert_element_type.191
  476.2 3.3 convert_element_type.189
  479.5 31.7 %reduce-scatter.5.cloned.1.call-done = bf16[128,2048]{1,0:T(8,128)(2,1)} async-done(((bf16[1024,2048]{1,0:T(8,128)(2,1)}), bf16[128,2048]{1,0:T(8,128)(2,1)}) %reduce-scatter.5.cloned.1.call-update) | async-done | bytes 524304 | tf_op jit(solution)/shard_map/reduce_scatter | solution.py:232
  512.9 39.7 %all-reduce = (f32[2048]{0:T(1024)}, f32[2048]{0:T(1024)}) all-reduce(f32[2048]{0:T(1024)S(1)} %get-tuple-element.174, f32[2048]{0:T(1024)S(1)} %get-tuple-element.177), channel_id=1, replica_groups=mesh['rows'=4,'tp'=8] {'rows','tp'}, use_global_device_ids=true, to_apply=%region_17.18 | all-reduce | flops 4096 | bytes 32768 | tf_op jit(solution)/shard_map/psum | solution.py:247
  552.6 10.7 %reduce-scatter.3.cloned.1.call-done = bf16[128,2048]{1,0:T(8,128)(2,1)} async-done(((bf16[1024,2048]{1,0:T(8,128)(2,1)}), bf16[128,2048]{1,0:T(8,128)(2,1)}) %reduce-scatter.3.cloned.1.call-update) | async-done | bytes 524304 | tf_op jit(solution)/shard_map/reduce_scatter | solution.py:195
  563.3 3.3 fusion.77
  566.7 3.3 convert_element_type.190
  570.0 82.2 %all-reduce.15.cloned.1.call-done = bf16[3,256,2048]{2,1,0:T(8,128)(2,1)} async-done(((bf16[3,256,2048]{2,1,0:T(8,128)(2,1)}), bf16[3,256,2048]{2,1,0:T(8,128)(2,1)}) %all-reduce.15.cloned.1.call-update) | async-done | bytes 3145744 | tf_op jit(solution)/shard_map/psum | solution.py:150
  652.1 5.4 convert_element_type.186
  (194 shorter events, 65.0 us)
Async XLA Ops:
  7.2 56.4 %copy-start = (bf16[3,256,2048]{2,1,0:T(8,128)(2,1)S(1)}, bf16[3,256,2048]{2,1,0:T(8,128)(2,1)}, u32[]{:S(2)}) copy-start(bf16[3,256,2048]{2,1,0:T(8,128)(2,1)} %param.18) | copy-start | bytes 9437188
  7.2 56.4 %all-gather.3.cloned.1.call-start = ((), (), s32[]{:S(2)}) async-start(), calls=%async_computation.2 | async-start | bytes 4718592 | tf_op jit(solution)/shard_map/all_gather | solution.py:182
  8.6 2.7 copy-start.23
  13.6 97.5 %all-gather.5.cloned.1.call-start = ((), (), s32[]{:S(2)}) async-start(), calls=%async_computation.4 | async-start | bytes 4718592 | tf_op jit(solution)/shard_map/all_gather | solution.py:188
  14.4 196.4 %all-reduce.7.cloned.1.call-start = ((), (), s32[]{:S(2)}) async-start(), calls=%async_computation.6 | async-start | bytes 5767168 | tf_op jit(solution)/shard_map/psum | solution.py:150
  63.6 8.6 %copy-start.32 = (bf16[704,2048]{1,0:T(8,128)(2,1)S(1)}, bf16[704,2048]{1,0:T(8,128)(2,1)}, u32[]{:S(2)}) copy-start(bf16[704,2048]{1,0:T(8,128)(2,1)} %param.22) | copy-start | bytes 8650756
  69.0 3.3 copy-start.27
  111.1 6.5 copy-start.28
  111.1 6.5 copy-start.31
  111.1 6.5 copy-start.37
  117.6 6.8 %copy-start.30 = (bf16[1024,2048]{1,0:T(8,128)(2,1)S(1)}, bf16[1024,2048]{1,0:T(8,128)(2,1)}, u32[]{:S(2)}) copy-start(bf16[1024,2048]{1,0:T(8,128)(2,1)} %all-gather.5.cloned.1.call-done) | copy-start | bytes 12582916
  129.1 137.5 %all-reduce.9.cloned.1.call-start = ((), (), s32[]{:S(2)}) async-start(), calls=%async_computation.7 | async-start | bytes 2097152 | tf_op jit(solution)/shard_map/psum | solution.py:150
  137.6 2.4 copy-start.5
  140.0 3.6 copy-start.21
  150.7 3.6 copy-start.21
  210.8 164.3 %all-reduce.11.cloned.1.call-start = ((), (), s32[]{:S(2)}) async-start(), calls=%async_computation.8 | async-start | bytes 5767168 | tf_op jit(solution)/shard_map/psum | solution.py:150
  210.8 4.8 copy-start.29
  210.8 4.8 copy-start.36
  215.7 51.1 %copy-start.22 = (f32[2,4,512]{2,1,0:T(4,128)S(1)}, f32[2,4,512]{2,1,0:T(4,128)}, u32[]{:S(2)}) copy-start(f32[2,4,512]{2,1,0:T(4,128)} %get-tuple-element.433) | copy-start | bytes 49156
  266.6 191.5 %all-reduce.13.cloned.1.call-start = ((), (), s32[]{:S(2)}) async-start(), calls=%async_computation.9 | async-start | bytes 5767168 | tf_op jit(solution)/shard_map/psum | solution.py:150
  277.2 7.0 %slice-start = ((s8[8388608]{0:T(1024)(128)(4,1)}), s8[4194304]{0:T(1024)(128)(4,1)S(1)}, s32[]{:S(2)}) async-start(s8[8388608]{0:T(1024)(128)(4,1)} %bitcast.139), calls=%async_computation.11 | async-start | bytes 8388608 | tf_op jit(solution)/shard_map/while
  277.2 7.0 %slice-start.1 = ((s8[8388608]{0:T(1024)(128)(4,1)}), s8[4194304]{0:T(1024)(128)(4,1)S(1)}, s32[]{:S(2)}) async-start(s8[8388608]{0:T(1024)(128)(4,1)} %bitcast.139), calls=%async_computation.12 | async-start | bytes 8388608 | tf_op jit(solution)/shard_map/while
  277.2 7.0 %copy-start.3 = (pred[512,1024]{1,0:T(8,128)(4,1)S(1)}, pred[512,1024]{1,0:T(8,128)(4,1)}, u32[]{:S(2)}) copy-start(pred[512,1024]{1,0:T(8,128)(4,1)} %fusion.159) | copy-start | bytes 1572868 | tf_op jit(solution)/shard_map/while
  284.3 4.4 copy-start.2
  301.8 4.2 copy-start.4
  301.8 4.2 copy-start.6
  322.2 7.0 %slice-start = ((s8[8388608]{0:T(1024)(128)(4,1)}), s8[4194304]{0:T(1024)(128)(4,1)S(1)}, s32[]{:S(2)}) async-start(s8[8388608]{0:T(1024)(128)(4,1)} %bitcast.139), calls=%async_computation.11 | async-start | bytes 8388608 | tf_op jit(solution)/shard_map/while
  322.2 7.0 %slice-start.1 = ((s8[8388608]{0:T(1024)(128)(4,1)}), s8[4194304]{0:T(1024)(128)(4,1)S(1)}, s32[]{:S(2)}) async-start(s8[8388608]{0:T(1024)(128)(4,1)} %bitcast.139), calls=%async_computation.12 | async-start | bytes 8388608 | tf_op jit(solution)/shard_map/while
  322.2 7.0 %copy-start.3 = (pred[512,1024]{1,0:T(8,128)(4,1)S(1)}, pred[512,1024]{1,0:T(8,128)(4,1)}, u32[]{:S(2)}) copy-start(pred[512,1024]{1,0:T(8,128)(4,1)} %fusion.159) | copy-start | bytes 1572868 | tf_op jit(solution)/shard_map/while
  329.3 4.4 copy-start.2
  346.8 4.5 copy-start.4
  346.8 4.5 copy-start.6
  375.1 136.0 %reduce-scatter.5.cloned.1.call-start = ((), (), s32[]{:S(2)}) async-start(), calls=%async_computation.5 | async-start | bytes 4718592 | tf_op jit(solution)/shard_map/reduce_scatter | solution.py:232
  383.1 5.9 copy-start.33
  383.1 5.9 copy-start.35
  389.0 5.8 copy-start.13
  389.0 5.8 copy-start.14
  389.0 5.8 copy-start.15
  402.5 160.8 %reduce-scatter.3.cloned.1.call-start = ((), (), s32[]{:S(2)}) async-start(), calls=%async_computation.3 | async-start | bytes 4718592 | tf_op jit(solution)/shard_map/reduce_scatter | solution.py:195
  402.8 6.0 copy-start.12
  402.9 6.0 copy-start.16
  412.2 239.9 %all-reduce.15.cloned.1.call-start = ((), (), s32[]{:S(2)}) async-start(), calls=%async_computation.10 | async-start | bytes 6291456 | tf_op jit(solution)/shard_map/psum | solution.py:150
  469.3 5.3 copy-start.17
  469.3 6.8 %copy-start.7 = (bf16[704,2048]{1,0:T(8,128)(2,1)S(1)}, bf16[704,2048]{1,0:T(8,128)(2,1)}, u32[]{:S(2)}) copy-start(bf16[704,2048]{1,0:T(8,128)(2,1)} %all-reduce.11.cloned.1.call-done) | copy-start | bytes 8650756
  476.1 35.0 %copy-start.19 = (f32[2048]{0:T(1024)S(1)}, f32[2048]{0:T(1024)}, u32[]{:S(2)}) copy-start(f32[2048]{0:T(1024)} %copy-done.18) | copy-start | bytes 24580
  476.1 35.0 %copy-start.24 = (f32[128]{0:T(128)S(1)}, f32[128]{0:T(128)}, u32[]{:S(2)}) copy-start(f32[128]{0:T(128)} %copy-done.23) | copy-start | bytes 1540
  476.2 35.0 %copy-start.26 = (f32[128]{0:T(128)S(1)}, f32[128]{0:T(128)}, u32[]{:S(2)}) copy-start(f32[128]{0:T(128)} %copy-done.25) | copy-start | bytes 1540
  563.3 3.3 copy-start.8
  (11 other events, 17.4 us)
Sparse Core Ops, SparseCore 0:
  13.7 49.8 all-gather.2
  65.2 45.8 all-gather.4
  129.2 81.5 all-reduce.6
  214.0 52.5 all-reduce.8
  270.4 82.7 all-reduce.10
  375.2 82.8 all-reduce.12
  461.1 49.9 reduce-scatter.4
  514.1 49.1 reduce-scatter.2
  566.7 85.3 all-reduce.14

commit v2 on v0

v2 whole, which is shorter than its diff:
```python
import functools
import jax
import jax.numpy as jnp
from jax import lax
from jax.experimental import pallas as pl
from jax.experimental.pallas import tpu as pltpu
from jax.sharding import PartitionSpec as P

HEAD = 64
ROT = 16
MASKED = -1e30
EPSILON = 1e-05
VMEM = 60 * 1024 * 1024


def dot_rows(a, b):
    return lax.dot_general(a, b, (((1,), (0,)), ((), ())), preferred_element_type=jnp.float32)


def dot_lanes(a, b):
    return lax.dot_general(a, b, (((1,), (1,)), ((), ())), preferred_element_type=jnp.float32)


def dot_tall(a, b):
    return lax.dot_general(a, b, (((0,), (0,)), ((), ())), preferred_element_type=jnp.float32)


def turn(values, tables, sign):
    half = ROT // 2
    width = values.shape[1]
    up = pltpu.roll(values, width - half, 1)
    down = pltpu.roll(values, half, 1)
    return values * tables[0] + sign * (up * tables[1] + down * tables[2])


def of_head(head, shape):
    return lax.broadcasted_iota(jnp.int32, shape, 1) // HEAD == head


def over_blocks(row_len, block, body):
    longest = row_len // 2
    blocks = row_len // block
    if blocks <= 8:
        for index in range(blocks):
            first = index * block
            start = max(0, first + block - (longest + block))
            body(first, start, first + block - start)
    else:
        size = longest + block

        def step(index, carry):
            first = pl.multiple_of(index * block, block)
            start = pl.multiple_of(jnp.maximum(first - longest, 0), block)
            body(first, start, size)
            return carry

        lax.fori_loop(0, blocks, step, 0)


def mask_of(seg_col, seg_row, first, start, block, size):
    rows = first + lax.broadcasted_iota(jnp.int32, (block, size), 0)
    keys = start + lax.broadcasted_iota(jnp.int32, (block, size), 1)
    same = seg_col[pl.ds(first, block), 0:1] == seg_row[0:1, pl.ds(start, size)]
    return jnp.where(same & (keys <= rows), 0.0, MASKED)


def forward_kernel(
    heads, lines, tables, seg_col, seg_row, query, key, value, context, context_t, logsum
):
    row_len, width = query.shape
    block = 256
    scale = HEAD ** (-0.5)
    query[...] = (turn(lines[:, 0:width], tables, 1.0).astype(jnp.bfloat16)) * jnp.bfloat16(scale)
    key[...] = turn(lines[:, width : 2 * width], tables, 1.0).astype(jnp.bfloat16)
    value[...] = lines[:, 2 * width : 3 * width].astype(jnp.bfloat16)

    def one_block(first, start, size):
        bias = mask_of(seg_col, seg_row, first, start, block, size)
        here = query[pl.ds(first, block), :]
        keys = key[pl.ds(start, size), :]
        values = value[pl.ds(start, size), :]
        total = jnp.zeros((block, width), jnp.float32)
        lane = lax.broadcasted_iota(jnp.int32, (block, 128), 1)
        sums = jnp.zeros((block, 128), jnp.float32)
        for head in range(heads):
            mine = of_head(head, (block, width))
            scores = dot_lanes(jnp.where(mine, here, jnp.bfloat16(0)), keys) + bias
            highest = jnp.max(scores, axis=1, keepdims=True)
            raised = jnp.exp(scores - highest)
            amount = jnp.sum(raised, axis=1, keepdims=True)
            weights = (raised * (1.0 / amount)).astype(jnp.bfloat16)
            total = jnp.where(mine, dot_rows(weights, values), total)
            sums = jnp.where(lane == head, highest + jnp.log(amount), sums)
        context[pl.ds(first, block), :] = total.astype(jnp.bfloat16)
        context_t[:, pl.ds(first, block)] = total.T.astype(jnp.bfloat16)
        logsum[pl.ds(first, block), :] = sums

    over_blocks(row_len, block, one_block)


def attend_forward(lines, tables, seg_col, seg_row, heads):
    row_len, width = lines.shape[0], lines.shape[1] // 3
    low = jax.ShapeDtypeStruct((row_len, width), jnp.bfloat16)
    return pl.pallas_call(
        functools.partial(forward_kernel, heads),
        out_shape=(
            low,
            low,
            low,
            low,
            jax.ShapeDtypeStruct((width, row_len), jnp.bfloat16),
            jax.ShapeDtypeStruct((row_len, 128), jnp.float32),
        ),
        compiler_params=pltpu.CompilerParams(vmem_limit_bytes=VMEM),
        cost_estimate=cost(
            heads * row_len * row_len * 256 * 2, 30 * row_len * width, heads * row_len * row_len // 2
        ),
        name="attend_forward",
    )(lines, tables, seg_col, seg_row)


def backward_kernel(
    heads,
    query,
    key,
    value,
    context_grad,
    logsum,
    tables,
    seg_col,
    seg_row,
    lines_low,
    lines_low_t,
    bias_grad,
    key_grad,
    value_grad,
):
    row_len, width = query.shape
    block = 256
    scale = HEAD ** (-0.5)
    key_grad[...] = jnp.zeros_like(key_grad)
    value_grad[...] = jnp.zeros_like(value_grad)
    bias_grad[...] = jnp.zeros_like(bias_grad)

    def put(part, first, grads):
        low = grads.astype(jnp.bfloat16)
        wide = low.astype(jnp.float32)
        columns = slice(part * width, (part + 1) * width)
        lines_low[pl.ds(first, block), columns] = low
        lines_low_t[columns, pl.ds(first, block)] = wide.T.astype(jnp.bfloat16)
        bias_grad[0:1, columns] += jnp.sum(wide, axis=0, keepdims=True)

    def one_block(first, start, size):
        bias = mask_of(seg_col, seg_row, first, start, block, size)
        here = query[pl.ds(first, block), :]
        grad_here = context_grad[pl.ds(first, block), :]
        keys = key[pl.ds(start, size), :]
        values = value[pl.ds(start, size), :]
        sums = logsum[pl.ds(first, block), :]
        total = jnp.zeros((block, width), jnp.float32)
        for head in range(heads):
            mine = of_head(head, (block, width))
            asked = jnp.where(mine, here, jnp.bfloat16(0))
            pulled = jnp.where(mine, grad_here, jnp.bfloat16(0))
            scores = dot_lanes(asked, keys) + bias
            probs = jnp.exp(scores - sums[:, head : head + 1])
            prob_grad = dot_lanes(pulled, values)
            value_grad[pl.ds(start, size), :] += dot_tall(probs.astype(jnp.bfloat16), pulled)
            inner = jnp.sum(probs * prob_grad, axis=1, keepdims=True)
            score_low = (probs * (prob_grad - inner)).astype(jnp.bfloat16)
            total = jnp.where(mine, dot_rows(score_low, keys), total)
            key_grad[pl.ds(start, size), :] += dot_tall(score_low, asked)
        here_tables = [tables[part, pl.ds(first, block), :] for part in range(3)]
        put(0, first, turn(total * scale, here_tables, -1.0))

    over_blocks(row_len, block, one_block)
    for index in range(row_len // block):
        first = index * block
        here_tables = [tables[part, pl.ds(first, block), :] for part in range(3)]
        put(1, first, turn(key_grad[pl.ds(first, block), :], here_tables, -1.0))
        put(2, first, value_grad[pl.ds(first, block), :])


def attend_backward(query, key, value, context_grad, logsum, tables, seg_col, seg_row, heads):
    row_len, width = query.shape
    return pl.pallas_call(
        functools.partial(backward_kernel, heads),
        out_shape=(
            jax.ShapeDtypeStruct((row_len, 3 * width), jnp.bfloat16),
            jax.ShapeDtypeStruct((3 * width, row_len), jnp.bfloat16),
            jax.ShapeDtypeStruct((8, 3 * width), jnp.float32),
        ),
        scratch_shapes=[
            pltpu.VMEM((row_len, width), jnp.float32),
            pltpu.VMEM((row_len, width), jnp.float32),
        ],
        compiler_params=pltpu.CompilerParams(vmem_limit_bytes=VMEM),
        cost_estimate=cost(
            5 * heads * row_len * row_len * 256, 30 * row_len * width, heads * row_len * row_len // 2
        ),
        name="attend_backward",
    )(query, key, value, context_grad, logsum, tables, seg_col, seg_row)


def layout(doc_lengths, row_len):
    ends = jnp.cumsum(doc_lengths[0])
    starts = ends - doc_lengths[0]
    places = jnp.arange(row_len, dtype=jnp.int32)
    segment = jnp.sum((places[:, None] >= ends[None, :]).astype(jnp.int32), axis=1)
    chosen = segment[:, None] == jnp.arange(ends.shape[0], dtype=jnp.int32)[None, :]
    first = jnp.sum(jnp.where(chosen, starts[None, :], 0), axis=1)
    return segment, places - first, segment < ends.shape[0] - 1


def turns(position, width):
    half = ROT // 2
    freq = 10000.0 ** (-(jnp.arange(half).astype(jnp.float32) * (2.0 / ROT)))
    angle = position.astype(jnp.float32)[:, None] * freq
    cosine, sine = jnp.cos(angle), jnp.sin(angle)
    rest = jnp.zeros((position.shape[0], HEAD - ROT), jnp.float32)
    none = jnp.zeros_like(sine)
    parts = (
        jnp.concatenate([cosine, cosine, rest + 1.0], axis=1),
        jnp.concatenate([-sine, none, rest], axis=1),
        jnp.concatenate([none, sine, rest], axis=1),
    )
    return jnp.stack([jnp.tile(part, (1, width // HEAD)) for part in parts])


def cost(flops, moved, transcendentals=0):
    return pl.CostEstimate(
        flops=int(flops), bytes_accessed=int(moved), transcendentals=int(transcendentals)
    )


def weight_kernel(count, order, *refs):
    lhs, rhs, (send, keep) = refs[:count], refs[count], refs[count + 1 :]
    step = pl.program_id(0)
    first = 0
    for part in lhs:
        rows = part.shape[0]
        term = dot_rows(part[...], rhs[...]).astype(jnp.bfloat16)

        @pl.when(step < 2)
        def _(first=first, rows=rows, term=term):
            send[first : first + rows, :] = term

        @pl.when(step >= 2)
        def _(first=first, rows=rows, term=term):
            keep[first : first + rows, :] = term

        first += rows


def weight_terms(lhs, rhs, base, bit, narrow):
    rows = sum(part.shape[0] for part in lhs)
    tokens = rhs.shape[0]
    order = base + jnp.stack([2 * (1 - bit), 2 * (1 - bit) + 1, 2 * bit, 2 * bit + 1])
    half = jax.ShapeDtypeStruct((rows, 2 * narrow), jnp.bfloat16)
    return pl.pallas_call(
        functools.partial(weight_kernel, len(lhs)),
        grid_spec=pltpu.PrefetchScalarGridSpec(
            num_scalar_prefetch=1,
            grid=(4,),
            in_specs=[
                *(pl.BlockSpec(part.shape, lambda step, order: (0, 0)) for part in lhs),
                pl.BlockSpec((tokens, narrow), lambda step, order: (0, order[step])),
            ],
            out_specs=[
                pl.BlockSpec((rows, narrow), lambda step, order: (0, jnp.minimum(step, 1))),
                pl.BlockSpec((rows, narrow), lambda step, order: (0, jnp.maximum(step - 2, 0))),
            ],
        ),
        out_shape=(half, half),
        compiler_params=pltpu.CompilerParams(vmem_limit_bytes=VMEM),
        cost_estimate=cost(
            2 * rows * tokens * 4 * narrow,
            2 * (rows * tokens + tokens * 4 * narrow + rows * 4 * narrow),
        ),
        name="weight_terms",
    )(order.astype(jnp.int32), *lhs, rhs)


def join_kernel(order, keep, came, send, mine):
    total = keep[...] + came[...]

    @pl.when(pl.program_id(1) == 0)
    def _():
        send[...] = total

    @pl.when(pl.program_id(1) == 1)
    def _():
        mine[...] = total


def join_terms(keep, came, bit):
    rows, narrow = keep.shape[0], keep.shape[1] // 2
    tall = rows // 4 if rows % 64 == 0 else rows
    order = jnp.stack([1 - bit, bit]).astype(jnp.int32)
    part = jax.ShapeDtypeStruct((rows, narrow), jnp.bfloat16)
    return pl.pallas_call(
        join_kernel,
        grid_spec=pltpu.PrefetchScalarGridSpec(
            num_scalar_prefetch=1,
            grid=(rows // tall, 2),
            in_specs=[
                pl.BlockSpec((tall, narrow), lambda block, step, order: (block, order[step])),
                pl.BlockSpec((tall, narrow), lambda block, step, order: (block, order[step])),
            ],
            out_specs=[
                pl.BlockSpec((tall, narrow), lambda block, step, order: (block, 0)),
                pl.BlockSpec((tall, narrow), lambda block, step, order: (block, 0)),
            ],
        ),
        out_shape=(part, part),
        compiler_params=pltpu.CompilerParams(vmem_limit_bytes=VMEM),
        cost_estimate=cost(rows * narrow, 12 * rows * narrow),
        name="join_terms",
    )(order, keep, came)


def place_kernel(count, order, *refs):
    pieces, outs = refs[:count], refs[count:]
    step = pl.program_id(0)
    for index, piece in enumerate(pieces):

        @pl.when(step == index)
        def _(piece=piece):
            first = 0
            for out in outs:
                rows = out.shape[0]
                out[...] = piece[first : first + rows, :].astype(jnp.float32)
                first += rows


def place_pieces(pieces, order, sizes):
    count = len(pieces)
    rows, narrow = pieces[0].shape
    return pl.pallas_call(
        functools.partial(place_kernel, count),
        grid_spec=pltpu.PrefetchScalarGridSpec(
            num_scalar_prefetch=1,
            grid=(count,),
            in_specs=[pl.BlockSpec((rows, narrow), lambda step, order: (0, 0))] * count,
            out_specs=[
                pl.BlockSpec((size, narrow), lambda step, order: (0, order[step]))
                for size in sizes
            ],
        ),
        out_shape=[jax.ShapeDtypeStruct((size, count * narrow), jnp.float32) for size in sizes],
        compiler_params=pltpu.CompilerParams(vmem_limit_bytes=VMEM),
        cost_estimate=cost(rows * narrow * count, 6 * rows * narrow * count),
        name="place_pieces",
    )(order.astype(jnp.int32), *pieces)


NEAR = [(0, 1), (1, 0), (2, 3), (3, 2)]
FAR = [(0, 2), (2, 0), (1, 3), (3, 1)]


def sum_half(lhs, rhs, base, pairs, bits, narrow):
    (first, second), (bit, other) = pairs, bits
    send, keep = weight_terms(lhs, rhs, base, bit, narrow)
    came = lax.ppermute(send, "rows", first)
    send, mine = join_terms(keep, came, other)
    mine = mine + lax.ppermute(send, "rows", second)
    across = lax.ppermute(mine, "rows", second)
    return [
        mine,
        across,
        lax.ppermute(mine, "rows", first),
        lax.ppermute(across, "rows", first),
    ]


def sum_over_rows(lhs, halves, bases, narrow):
    row = lax.axis_index("rows")
    near, far = row % 2, row // 2
    left = sum_half(lhs, halves[0], bases[0], (NEAR, FAR), (near, far), narrow)
    right = sum_half(lhs, halves[1], bases[1], (FAR, NEAR), (far, near), narrow)
    order = []
    for base, bit, other in ((0, near, far), (4, far, near)):
        for a, b in ((bit, other), (bit, 1 - other), (1 - bit, other), (1 - bit, 1 - other)):
            order.append(base + 2 * a + b)
    return place_pieces(left + right, jnp.stack(order), [part.shape[0] for part in lhs])


def standardize(values):
    centre = jnp.mean(values, axis=1, keepdims=True)
    centred = values - centre
    spread = jnp.mean(centred * centred, axis=1, keepdims=True)
    inverse = lax.rsqrt(spread + EPSILON)
    return (centred * inverse, inverse)


def product(a, b):
    return jnp.dot(a, b, preferred_element_type=jnp.float32)


def widen(values, heads_width, width):
    if heads_width == width:
        return values
    groups = values.shape[-1] // heads_width
    split = values.reshape(*values.shape[:-1], groups, heads_width)
    spare = [(0, 0)] * (split.ndim - 1) + [(0, width - heads_width)]
    return jnp.pad(split, spare).reshape(*values.shape[:-1], groups * width)


def per_device(
    block_input,
    norm_gain,
    norm_bias,
    qkv_weight,
    qkv_bias,
    out_weight,
    gate_weight,
    up_weight,
    down_weight,
    cotangent,
    doc_lengths,
):
    shard, features = block_input.shape
    group = lax.axis_size("tp")
    tokens = shard * group
    width = qkv_weight.shape[1]
    heads = width // HEAD
    padded = max(width, 128)
    half = features // 2
    me = lax.axis_index("tp")
    segment, position, live = layout(doc_lengths, tokens)
    live_mine = lax.dynamic_slice_in_dim(live, me * shard, shard)[:, None]
    input_wide = block_input.astype(jnp.float32)
    gain = norm_gain.astype(jnp.float32)
    shift = norm_bias.astype(jnp.float32)
    normed, inverse = standardize(input_wide)
    normed_low = (normed * gain + shift).astype(jnp.bfloat16)
    hidden_in = lax.all_gather(normed_low, "tp", axis=0, tiled=True)
    grad_mine = jnp.where(live_mine, cotangent, jnp.zeros_like(cotangent))
    grad_mine, _ = lax.optimization_barrier((grad_mine, hidden_in))
    grad_left = lax.all_gather(grad_mine[:, :half], "tp", axis=0, tiled=True)
    grad_right_mine, _ = lax.optimization_barrier((grad_mine[:, half:], grad_left))
    grad_right = lax.all_gather(grad_right_mine, "tp", axis=0, tiled=True)
    tables = turns(position, padded)
    seg_col = jnp.broadcast_to(segment[:, None], (tokens, 128))
    seg_row = jnp.broadcast_to(segment[None, :], (8, tokens))

    gate = jnp.einsum("td,fd->tf", hidden_in, gate_weight, preferred_element_type=jnp.float32)
    up = jnp.einsum("td,fd->tf", hidden_in, up_weight, preferred_element_type=jnp.float32)
    sigmoid = jax.nn.sigmoid(gate)
    mixed = (gate * sigmoid * up).astype(jnp.bfloat16)
    projection = qkv_weight.reshape(3 * width, features)
    lines = jnp.einsum("td,ed->te", hidden_in, projection, preferred_element_type=jnp.float32)
    lines = lines + qkv_bias.astype(jnp.float32).reshape(1, 3 * width)
    query, key, value, context, context_t, logsum = attend_forward(
        widen(lines, width, padded), tables, seg_col, seg_row, heads
    )
    context, context_t = context[:, :width], context_t[:width]
    down_grad, out_grad = sum_over_rows(
        [mixed.T, context_t], [grad_left, grad_right], [0, 0], features // 8
    )
    merged = product(context, out_weight) + product(mixed, down_weight)
    merged = lax.psum_scatter(
        merged.astype(jnp.bfloat16), "tp", scatter_dimension=0, tiled=True
    ).astype(jnp.float32)
    output = (input_wide + jnp.where(live_mine, merged, 0.0)).astype(jnp.bfloat16)

    def pulled(weight):
        return product(grad_left, weight[:, :half].T) + product(grad_right, weight[:, half:].T)

    mixed_grad = pulled(down_weight)
    gate_low = (mixed_grad * up * sigmoid * (1.0 + gate * (1.0 - sigmoid))).astype(jnp.bfloat16)
    up_low = (mixed_grad * gate * sigmoid).astype(jnp.bfloat16)
    gate_grad, up_grad = sum_over_rows(
        [gate_low.T, up_low.T], [hidden_in, hidden_in], [0, 4], features // 8
    )
    context_grad = pulled(out_weight).astype(jnp.bfloat16)
    lines_low, lines_low_t, bias_grad = attend_backward(
        query,
        key,
        value,
        widen(context_grad, width, padded),
        logsum,
        tables,
        seg_col,
        seg_row,
        heads,
    )
    lines_low = lines_low.reshape(tokens, 3, padded)[:, :, :width].reshape(tokens, 3 * width)
    lines_low_t = lines_low_t.reshape(3, padded, tokens)[:, :width].reshape(3 * width, tokens)
    bias_grad = bias_grad[0].reshape(3, padded)[:, :width]
    (qkv_grad,) = sum_over_rows([lines_low_t], [hidden_in, hidden_in], [0, 4], features // 8)
    term = product(lines_low, projection) + product(gate_low, gate_weight)
    term = term + product(up_low, up_weight)
    normed_grad = lax.psum_scatter(
        term.astype(jnp.bfloat16), "tp", scatter_dimension=0, tiled=True
    ).astype(jnp.float32)
    scaled = normed_grad * gain
    input_grad = inverse * (
        scaled
        - jnp.mean(scaled, axis=1, keepdims=True)
        - normed * jnp.mean(scaled * normed, axis=1, keepdims=True)
    )
    input_grad = input_grad + cotangent.astype(jnp.float32)
    bias_slots = lax.dynamic_update_slice(
        jnp.zeros((3, group * width), jnp.float32), bias_grad, (0, me * width)
    )
    small = jnp.concatenate(
        [
            jnp.sum(normed_grad * normed, axis=0),
            jnp.sum(normed_grad, axis=0),
            bias_slots.reshape(-1),
        ]
    )
    small = lax.psum(small, ("rows", "tp"))
    bias_slots = small[2 * features :].reshape(3, group * width)
    return (
        output,
        input_grad,
        small[:features],
        small[features : 2 * features],
        qkv_grad.reshape(3, width, features),
        lax.dynamic_slice(bias_slots, (0, me * width), (3, width)),
        out_grad,
        gate_grad,
        up_grad,
        down_grad,
    )


def solution(mesh):
    placed = (
        P(("rows", "tp"), None),
        P(),
        P(),
        P(None, "tp", None),
        P(None, "tp"),
        P("tp", None),
        P("tp", None),
        P("tp", None),
        P("tp", None),
        P(("rows", "tp"), None),
        P("rows", None),
    )
    return jax.shard_map(
        per_device,
        mesh=mesh,
        in_specs=placed,
        out_specs=(
            P(("rows", "tp"), None),
            P(("rows", "tp"), None),
            P(),
            P(),
            P(None, "tp", None),
            P(None, "tp"),
            P("tp", None),
            P("tp", None),
            P("tp", None),
            P("tp", None),
        ),
        check_vma=False,
    )
```

time: 930 us -> 521 us (0.56)
  waiting for transfers between devices: 608 us -> 186 us
  Pallas kernels: 0 us -> 136 us
  matrix products: 141 us -> 62.1 us
  local copies, waits for them, and re-layouts: 61.7 us -> 22.2 us
  starting transfers between devices: 0.61 us -> 30.1 us
  other arithmetic: 37.8 us -> 26.8 us
  blocking collectives: 50.3 us -> 39.6 us
    psum x1 -> x0, waiting for transfers between devices: 456 us -> none  [per_device(): lax.psum((qkv_grad, qkv_bias_grad, out_grad, gate_grad, up_grad, down_gra...]
    pallas_call x0 -> x17, Pallas kernels: none -> 136 us  [the longest x6 51.2 us: weight_terms(): pl.pallas_call(functools.partial(weight_kernel, len(lhs)), grid_spec=pltp...]
    ppermute x0 -> x30, waiting for transfers between devices: none -> 124 us  [the longest x6 43.2 us: sum_half(): lax.ppermute(across, 'rows', first)]
    reduce_scatter x2, waiting for transfers between devices: 87.6 us -> 0.01 us  [the longest x1 0.01 us: per_device(): lax.psum_scatter(term.astype(jnp.bfloat16), 'tp', scatter_dimension=0, ti...]
    dot_general x29 -> x12, matrix products: 141 us -> 62.1 us  [the longest x9 44 us: product(): return jnp.dot(a, b, preferred_element_type=jnp.float32)]
    ppermute x0 -> x30, starting transfers between devices: none -> 28.9 us  [the longest x6 7.47 us: sum_half(): lax.ppermute(across, 'rows', first)]
    dynamic_update_slice x4 -> x1, local copies, waits for them, and re-layouts: 23.5 us -> 0.01 us  [per_device(): lax.dynamic_update_slice(jnp.zeros((3, group * width), jnp.float32), bias...]
    unnamed x68 -> x102, local copies, waits for them, and re-layouts: 18.8 us -> 3.94 us
  transfers between devices with their start and end apart: 5 -> 35, of which waited for: 5 -> 10; matrix products, arithmetic and copies ran while one was open for 8% -> 13% of each run, Pallas kernels for 0% -> 23%
where the time goes in v2:
time: 521 us; the launch traced here: 517 us
  waiting for transfers between devices  186 us (36%)
  Pallas kernels  136 us (26%)
  matrix products  62.1 us (12%)
  blocking collectives  39.6 us (8%)
  starting transfers between devices  30.1 us (6%)
  other arithmetic  26.8 us (5%)
  local copies, waits for them, and re-layouts  22.2 us (4%)
  between operations  14.7 us (3%)
    pallas_call x6, Pallas kernels, weight_terms(): pl.pallas_call(functools.partial(weight_kernel, len(lhs)), grid_spec=pltp...  51.2 us
    all_gather x1, waiting for transfers between devices, per_device(): hidden_in = lax.all_gather(normed_low, 'tp', axis=0, tiled=True)  46.4 us
    dot_general x9, matrix products, product(): return jnp.dot(a, b, preferred_element_type=jnp.float32)  44 us
    ppermute x6, waiting for transfers between devices, sum_half(): lax.ppermute(across, 'rows', first)  43.2 us
    ppermute x6, waiting for transfers between devices, sum_half(): across = lax.ppermute(mine, 'rows', second)  42 us
    psum x1, blocking collectives, per_device(): small = lax.psum(small, ('rows', 'tp'))  39.6 us
    ppermute x6, waiting for transfers between devices, sum_half(): came = lax.ppermute(send, 'rows', first)  38.9 us
    pallas_call x6, Pallas kernels, join_terms(): pl.pallas_call(join_kernel, grid_spec=pltpu.PrefetchScalarGridSpec(num_sc...  35.8 us
  transfers between devices with their start and end apart: 35, of which 10 were waited for; matrix products, arithmetic and copies ran while one was open for 13% of the time, Pallas kernels for 23%

profile of v2, /device:TPU:0, one launch (start us, length us, event | category | flops | bytes accessed | tf_op | source)
XLA Modules:
  0.0 516.7 jit_solution(1981261395797501615)
XLA Ops:
  12.0 2.2 fusion.27
  15.9 1.9 broadcast_select_fusion
  17.8 46.4 %all-gather.4.cloned.1.call-done.refs_1_.refs_2_ = bf16[1024,2048]{1,0:T(8,128)(2,1)} async-done(((bf16[128,2048]{1,0:T(8,128)(2,1)}), bf16[1024,2048]{1,0:T(8,128)(2,1)}) %all-gather.4.cloned.1.call-update) | async-done | bytes 4194320 | tf_op jit(solution)/shard_map/all_gather | solution.py:437
  64.2 1.9 fusion.43
  68.6 2.5 copy.26
  71.1 2.0 tile.26
  73.1 2.5 copy.25
  76.8 2.5 copy.24
  79.3 14.9 %all-gather.6.cloned.1.call-done.refs_2_ = bf16[1024,1024]{1,0:T(8,128)(2,1)} async-done(((bf16[128,1024]{1,0:T(8,128)(2,1)}), bf16[1024,1024]{1,0:T(8,128)(2,1)}) %all-gather.6.cloned.1.call-update) | async-done | bytes 2097168 | tf_op jit(solution)/shard_map/all_gather | solution.py:440
  94.8 3.9 pad_maximum_fusion.tables
  98.7 5.1 convolution_add_fusion.lines
  105.5 10.7 %attend_forward.1 = (bf16[1024,256]{1,0:T(8,128)(2,1)}, bf16[1024,256]{1,0:T(8,128)(2,1)}, bf16[1024,256]{1,0:T(8,128)(2,1)}, bf16[1024,256]{1,0:T(8,128)(2,1)},...) custom-call(f32[1024,768]{1,0:T(8,128)} %convolution_add_fusion.lines, f32[3,1024,256]{2,1,0:T(8,128)} %pad_maximum_fusion.tables, ...), custom_call_target="tpu_custom_call" | custom-call | flops 2147483648 | bytes 7864320 | tf_op jit(solution)/shard_map/attend_forward/pallas_call | solution.py:104
  116.2 8.0 %fusion.45 = f32[1024,704]{0,1:T(8,128)} fusion(bf16[1024,2048]{1,0:T(8,128)(2,1)} %all-gather.4.cloned.1.call-done.refs_1_.refs_2_, bf16[704,2048]{1,0:T(8,128)(2,1)} %param.17), kind=kOutput, calls=%fused_computation.94 | convolution fusion | flops 2952790016 | bytes 9961472 | tf_op jit(solution)/shard_map/td,fd->tf/dot_general | solution.py:447
  124.2 4.9 fusion.46
  131.2 3.3 fusion.16
  134.5 3.6 fusion.21.context_grad
  138.1 15.3 %attend_backward.1 = (bf16[1024,768]{1,0:T(8,128)(2,1)}, bf16[768,1024]{1,0:T(8,128)(2,1)}, f32[8,768]{1,0:T(8,128)}) custom-call(bf16[1024,256]{1,0:T(8,128)(2,1)} %get-tuple-element.50.query, bf16[1024,256]{1,0:T(8,128)(2,1)} %get-tuple-element.51.key, bf16[1024,256]{1,0:T(8,128)(2,1)} %get-tuple-element.52.value, bf16[1024,256]{1,0:T(8,128)(2,1)} %fusion.21.context_grad, ...), custom_call_target="tpu_custom_call" | custom-call | flops 5368709120 | bytes 7864320 | tf_op jit(solution)/shard_map/attend_backward/pallas_call | solution.py:186
  153.4 5.0 fusion.47
  158.8 4.5 fusion.4
  164.9 6.3 %fusion.14 = f32[1024,2048]{1,0:T(8,128)} fusion(bf16[704,2048]{1,0:T(8,128)(2,1)S(1)} %copy-done.40, f32[1024,704]{0,1:T(8,128)S(1)} %copy-done.47, f32[1024,704]{0,1:T(8,128)S(1)} %get-tuple-element.108, f32[1024,704]{0,1:T(8,128)S(1)} %copy-done.50), kind=kOutput, calls=%fused_computation.35 | convolution fusion | flops 2959998976 | bytes 19922944 | tf_op jit(solution)/shard_map/dot_general | solution.py:397
  171.2 9.7 %add_convert_fusion = bf16[1024,2048]{1,0:T(8,128)(2,1)} fusion(f32[1024,2048]{1,0:T(8,128)S(1)} %fusion.47, f32[1024,2048]{1,0:T(8,128)} %fusion.14, bf16[704,2048]{1,0:T(8,128)(2,1)S(1)} %copy-done.42, f32[1024,704]{0,1:T(8,128)} %copy-done.48, f32[1024,704]{0,1:T(8,128)} %fusion.45), kind=kOutput, calls=%fused_computation | convolution fusion | flops 2963406848 | bytes 29622272 | tf_op jit(solution)/shard_map/dot_general | solution.py:397
  181.4 6.6 %fusion.13 = f32[1024,2048]{1,0:T(8,128)S(1)} fusion(bf16[704,2048]{1,0:T(8,128)(2,1)} %param.19, f32[1024,704]{0,1:T(8,128)} %fusion.46, f32[1024,704]{0,1:T(8,128)} %fusion.45), kind=kOutput, calls=%fused_computation.34 | convolution fusion | flops 2957115392 | bytes 17039360 | tf_op jit(solution)/shard_map/dot_general | solution.py:397
  188.1 3.4 add_convert_fusion.1
  192.7 6.3 %weight_terms.6 = (bf16[768,512]{1,0:T(8,128)(2,1)}, bf16[768,512]{1,0:T(8,128)(2,1)}) custom-call(s32[4]{0:T(128)} %pad_add_fusion.1.order, bf16[768,1024]{1,0:T(8,128)(2,1)} %get-tuple-element.58.refs_0_, bf16[1024,2048]{1,0:T(8,128)(2,1)} %all-gather.4.cloned.1.call-done.refs_1_.refs_2_), custom_call_target="tpu_custom_call" | custom-call | flops 1610612736 | bytes 5242880 | tf_op jit(solution)/shard_map/weight_terms/pallas_call | solution.py:260
  200.5 8.0 %weight_terms.8 = (bf16[960,512]{1,0:T(8,128)(2,1)}, bf16[960,512]{1,0:T(8,128)(2,1)}) custom-call(s32[4]{0:T(128)} %pad_add_fusion.1.order, bf16[704,1024]{1,0:T(8,128)(2,1)} %get-tuple-element.96.refs_0_, bf16[256,1024]{1,0:T(8,128)(2,1)} %get-tuple-element.67.refs_1_, bf16[1024,1024]{1,0:T(8,128)(2,1)} %all-gather.6.cloned.1.call-done.refs_2_), custom_call_target="tpu_custom_call" | custom-call | flops 2013265920 | bytes 6029312 | tf_op jit(solution)/shard_map/weight_terms/pallas_call | solution.py:260
  209.0 11.3 %weight_terms.10 = (bf16[1408,512]{1,0:T(8,128)(2,1)}, bf16[1408,512]{1,0:T(8,128)(2,1)}) custom-call(s32[4]{0:T(128)} %pad_add_fusion.1.order, bf16[704,1024]{1,0:T(8,128)(2,1)} %get-tuple-element.95.refs_0_, bf16[704,1024]{1,0:T(8,128)(2,1)} %get-tuple-element.94.refs_1_, bf16[1024,2048]{1,0:T(8,128)(2,1)} %all-gather.4.cloned.1.call-done.refs_1_.refs_2_), custom_call_target="tpu_custom_call" | custom-call | flops 2952790016 | bytes 7864320 | tf_op jit(solution)/shard_map/weight_terms/pallas_call | solution.py:260
  221.8 8.0 %weight_terms.9 = (bf16[960,512]{1,0:T(8,128)(2,1)}, bf16[960,512]{1,0:T(8,128)(2,1)}) custom-call(s32[4]{0:T(128)} %get-tuple-element.93.order, bf16[704,1024]{1,0:T(8,128)(2,1)} %get-tuple-element.96.refs_0_, bf16[256,1024]{1,0:T(8,128)(2,1)} %get-tuple-element.67.refs_1_, bf16[1024,1024]{1,0:T(8,128)(2,1)} %all-gather.8.cloned.1.call-done.refs_2_), custom_call_target="tpu_custom_call" | custom-call | flops 2013265920 | bytes 6029312 | tf_op jit(solution)/shard_map/weight_terms/pallas_call | solution.py:260
  231.3 11.4 %weight_terms.11 = (bf16[1408,512]{1,0:T(8,128)(2,1)}, bf16[1408,512]{1,0:T(8,128)(2,1)}) custom-call(s32[4]{0:T(128)} %get-tuple-element.92.order, bf16[704,1024]{1,0:T(8,128)(2,1)} %get-tuple-element.95.refs_0_, bf16[704,1024]{1,0:T(8,128)(2,1)} %get-tuple-element.94.refs_1_, bf16[1024,2048]{1,0:T(8,128)(2,1)} %all-gather.4.cloned.1.call-done.refs_1_.refs_2_), custom_call_target="tpu_custom_call" | custom-call | flops 2952790016 | bytes 7864320 | tf_op jit(solution)/shard_map/weight_terms/pallas_call | solution.py:260
  243.2 6.3 %weight_terms.7 = (bf16[768,512]{1,0:T(8,128)(2,1)}, bf16[768,512]{1,0:T(8,128)(2,1)}) custom-call(s32[4]{0:T(128)} %get-tuple-element.92.order, bf16[768,1024]{1,0:T(8,128)(2,1)} %get-tuple-element.58.refs_0_, bf16[1024,2048]{1,0:T(8,128)(2,1)} %all-gather.4.cloned.1.call-done.refs_1_.refs_2_), custom_call_target="tpu_custom_call" | custom-call | flops 1610612736 | bytes 5242880 | tf_op jit(solution)/shard_map/weight_terms/pallas_call | solution.py:260
  251.5 5.6 %join_terms.6 = (bf16[768,256]{1,0:T(8,128)(2,1)}, bf16[768,256]{1,0:T(8,128)(2,1)}) custom-call(s32[2]{0:T(128)} %pad_add_fusion.order, bf16[768,512]{1,0:T(8,128)(2,1)} %get-tuple-element.59.keep, bf16[768,512]{1,0:T(8,128)(2,1)} %collective-permute-done.came), custom_call_target="tpu_custom_call" | custom-call | flops 196608 | bytes 2359296 | tf_op jit(solution)/shard_map/join_terms/pallas_call | solution.py:301
  257.8 5.9 %join_terms.8 = (bf16[960,256]{1,0:T(8,128)(2,1)}, bf16[960,256]{1,0:T(8,128)(2,1)}) custom-call(s32[2]{0:T(128)} %pad_add_fusion.order, bf16[960,512]{1,0:T(8,128)(2,1)} %get-tuple-element.68.keep, bf16[960,512]{1,0:T(8,128)(2,1)} %collective-permute-done.10.came), custom_call_target="tpu_custom_call" | custom-call | flops 245760 | bytes 2949120 | tf_op jit(solution)/shard_map/join_terms/pallas_call | solution.py:301
  263.6 38.9 %collective-permute-done.5.came = bf16[768,512]{1,0:T(8,128)(2,1)} collective-permute-done((bf16[768,512]{1,0:T(8,128)(2,1)}, bf16[768,512]{1,0:T(8,128)(2,1)}, u32[]{:S(2)}, u32[]{:S(2)}) %collective-permute-start.5) | collective-permute-done | bytes 786464 | tf_op jit(solution)/shard_map/ppermute | solution.py:364
  304.6 5.6 %join_terms.7 = (bf16[768,256]{1,0:T(8,128)(2,1)}, bf16[768,256]{1,0:T(8,128)(2,1)}) custom-call(s32[2]{0:T(128)} %pad_add_fusion.2.order, bf16[768,512]{1,0:T(8,128)(2,1)} %get-tuple-element.63.keep, bf16[768,512]{1,0:T(8,128)(2,1)} %collective-permute-done.5.came), custom_call_target="tpu_custom_call" | custom-call | flops 196608 | bytes 2359296 | tf_op jit(solution)/shard_map/join_terms/pallas_call | solution.py:301
  311.2 5.8 %join_terms.9 = (bf16[960,256]{1,0:T(8,128)(2,1)}, bf16[960,256]{1,0:T(8,128)(2,1)}) custom-call(s32[2]{0:T(128)} %pad_add_fusion.2.order, bf16[960,512]{1,0:T(8,128)(2,1)} %get-tuple-element.72.keep, bf16[960,512]{1,0:T(8,128)(2,1)} %copy-done.13), custom_call_target="tpu_custom_call" | custom-call | flops 245760 | bytes 2949120 | tf_op jit(solution)/shard_map/join_terms/pallas_call | solution.py:301
  318.3 6.3 %join_terms.10 = (bf16[1408,256]{1,0:T(8,128)(2,1)}, bf16[1408,256]{1,0:T(8,128)(2,1)}) custom-call(s32[2]{0:T(128)} %pad_add_fusion.order, bf16[1408,512]{1,0:T(8,128)(2,1)} %get-tuple-element.77.keep, bf16[1408,512]{1,0:T(8,128)(2,1)} %copy-done.12), custom_call_target="tpu_custom_call" | custom-call | flops 360448 | bytes 4325376 | tf_op jit(solution)/shard_map/join_terms/pallas_call | solution.py:301
  329.0 6.5 %join_terms.11 = (bf16[1408,256]{1,0:T(8,128)(2,1)}, bf16[1408,256]{1,0:T(8,128)(2,1)}) custom-call(s32[2]{0:T(128)} %pad_add_fusion.2.order, bf16[1408,512]{1,0:T(8,128)(2,1)} %get-tuple-element.81.keep, bf16[1408,512]{1,0:T(8,128)(2,1)} %copy-done.11), custom_call_target="tpu_custom_call" | custom-call | flops 360448 | bytes 4325376 | tf_op jit(solution)/shard_map/join_terms/pallas_call | solution.py:301
  338.9 10.8 %collective-permute-done.2.refs_1_ = bf16[768,256]{1,0:T(8,128)(2,1)} collective-permute-done((bf16[768,256]{1,0:T(8,128)(2,1)S(1)}, bf16[768,256]{1,0:T(8,128)(2,1)}, u32[]{:S(2)}, u32[]{:S(2)}) %collective-permute-start.2) | collective-permute-done | bytes 393248 | tf_op jit(solution)/shard_map/ppermute | solution.py:367
  352.4 11.4 %collective-permute-done.7.refs_5_ = bf16[768,256]{1,0:T(8,128)(2,1)S(1)} collective-permute-done((bf16[768,256]{1,0:T(8,128)(2,1)S(1)}, bf16[768,256]{1,0:T(8,128)(2,1)S(1)}, u32[]{:S(2)}, u32[]{:S(2)}) %collective-permute-start.7) | collective-permute-done | bytes 393248 | tf_op jit(solution)/shard_map/ppermute | solution.py:367
  368.8 3.4 collective-permute-done.4.refs_3_
  373.0 13.4 %collective-permute-done.9.refs_7_ = bf16[768,256]{1,0:T(8,128)(2,1)S(1)} collective-permute-done((bf16[768,256]{1,0:T(8,128)(2,1)S(1)}, bf16[768,256]{1,0:T(8,128)(2,1)S(1)}, u32[]{:S(2)}, u32[]{:S(2)}) %collective-permute-start.9) | collective-permute-done | bytes 393248 | tf_op jit(solution)/shard_map/ppermute | solution.py:372
  389.0 19.9 %collective-permute-done.17.refs_5_ = bf16[960,256]{1,0:T(8,128)(2,1)} collective-permute-done((bf16[960,256]{1,0:T(8,128)(2,1)S(1)}, bf16[960,256]{1,0:T(8,128)(2,1)}, u32[]{:S(2)}, u32[]{:S(2)}) %collective-permute-start.17) | collective-permute-done | bytes 491552 | tf_op jit(solution)/shard_map/ppermute | solution.py:367
  412.9 6.4 %collective-permute-done.14.refs_3_ = bf16[960,256]{1,0:T(8,128)(2,1)S(1)} collective-permute-done((bf16[960,256]{1,0:T(8,128)(2,1)S(1)}, bf16[960,256]{1,0:T(8,128)(2,1)S(1)}, u32[]{:S(2)}, u32[]{:S(2)}) %collective-permute-start.14) | collective-permute-done | bytes 491552 | tf_op jit(solution)/shard_map/ppermute | solution.py:372
  421.4 6.6 %place_pieces.3 = f32[768,2048]{1,0:T(8,128)} custom-call(s32[8]{0:T(128)} %stack.61.order, bf16[768,256]{1,0:T(8,128)(2,1)} %copy-done.9, bf16[768,256]{1,0:T(8,128)(2,1)} %collective-permute-done.2.refs_1_, bf16[768,256]{1,0:T(8,128)(2,1)} %copy-done.23, bf16[768,256]{1,0:T(8,128)(2,1)} %copy-done.26, bf16[768,256]{1,0:T(8,128)(2,1)} %copy-done.10, ...), custom_call_target="tpu_custom_call" | custom-call | flops 1572864 | bytes 9437184 | tf_op jit(solution)/shard_map/place_pieces/pallas_call | solution.py:339
  428.1 20.1 %collective-permute-done.19.refs_7_ = bf16[960,256]{1,0:T(8,128)(2,1)} collective-permute-done((bf16[960,256]{1,0:T(8,128)(2,1)}, bf16[960,256]{1,0:T(8,128)(2,1)}, u32[]{:S(2)}, u32[]{:S(2)}) %collective-permute-start.19) | collective-permute-done | bytes 491552 | tf_op jit(solution)/shard_map/ppermute | solution.py:372
  448.1 7.2 %place_pieces.4 = (f32[704,2048]{1,0:T(8,128)}, f32[256,2048]{1,0:T(8,128)}) custom-call(s32[8]{0:T(128)} %stack.61.order, bf16[960,256]{1,0:T(8,128)(2,1)} %copy-done.7, bf16[960,256]{1,0:T(8,128)(2,1)} %copy-done.17, bf16[960,256]{1,0:T(8,128)(2,1)} %copy-done.18, bf16[960,256]{1,0:T(8,128)(2,1)} %copy-done.22, bf16[960,256]{1,0:T(8,128)(2,1)} %copy-done.8, ...), custom_call_target="tpu_custom_call" | custom-call | flops 1966080 | bytes 11796480 | tf_op jit(solution)/shard_map/place_pieces/pallas_call | solution.py:339
  455.4 8.8 %place_pieces.5 = (f32[704,2048]{1,0:T(8,128)}, f32[704,2048]{1,0:T(8,128)}) custom-call(s32[8]{0:T(128)} %stack.61.order, bf16[1408,256]{1,0:T(8,128)(2,1)} %copy-done.2, bf16[1408,256]{1,0:T(8,128)(2,1)} %copy-done.14, bf16[1408,256]{1,0:T(8,128)(2,1)} %collective-permute-done.23.refs_2_, bf16[1408,256]{1,0:T(8,128)(2,1)} %collective-permute-done.24.refs_3_, ...), custom_call_target="tpu_custom_call" | custom-call | flops 2883584 | bytes 17301504 | tf_op jit(solution)/shard_map/place_pieces/pallas_call | solution.py:339
  465.9 39.6 %psum.7 = f32[10240]{0:T(1024)S(1)} all-reduce(f32[10240]{0:T(1024)S(1)} %pad_maximum_fusion.1), channel_id=1, replica_groups=mesh['rows'=4,'tp'=8] {'rows','tp'}, use_global_device_ids=true, to_apply=%region_11.12 | all-reduce | flops 10240 | bytes 81920 | tf_op jit(solution)/shard_map/psum | solution.py:514
  506.8 3.2 fusion.30
  (218 shorter events, 58.2 us)
Async XLA Ops:
  7.2 91.6 %copy-start = (bf16[3,256,2048]{2,1,0:T(8,128)(2,1)S(1)}, bf16[3,256,2048]{2,1,0:T(8,128)(2,1)}, u32[]{:S(2)}) copy-start(bf16[3,256,2048]{2,1,0:T(8,128)(2,1)} %param.14) | copy-start | bytes 9437188
  7.2 59.1 %copy-start.46 = (s32[1,8]{1,0:T(1,128)S(1)}, s32[1,8]{1,0:T(1,128)}, u32[]{:S(2)}) copy-start(s32[1,8]{1,0:T(1,128)} %param.21) | copy-start | bytes 100
  7.2 58.9 %copy-start.37 = (bf16[3,256]{1,0:T(4,128)(2,1)S(1)}, bf16[3,256]{1,0:T(4,128)(2,1)}, u32[]{:S(2)}) copy-start(bf16[3,256]{1,0:T(4,128)(2,1)} %param.15) | copy-start | bytes 4612
  7.2 57.0 %all-gather.4.cloned.1.call-start = ((), (), s32[]{:S(2)}) async-start(), calls=%async_computation.2 | async-start | bytes 4718592 | tf_op jit(solution)/shard_map/all_gather | solution.py:437
  14.2 80.0 %all-gather.6.cloned.1.call-start = ((), (), s32[]{:S(2)}) async-start(), calls=%async_computation.4 | async-start | bytes 2359296 | tf_op jit(solution)/shard_map/all_gather | solution.py:440
  66.1 68.4 %all-gather.8.cloned.1.call-start = ((), (), s32[]{:S(2)}) async-start(), calls=%async_computation.5 | async-start | bytes 2359296 | tf_op jit(solution)/shard_map/all_gather | solution.py:442
  94.3 369.9 %reduce-scatter.5.cloned.1.call-start = ((), (), s32[]{:S(2)}) async-start(), calls=%async_computation.6 | async-start | bytes 4718592 | tf_op jit(solution)/shard_map/reduce_scatter | solution.py:494
  181.0 325.8 %reduce-scatter.3.cloned.1.call-start = ((), (), s32[]{:S(2)}) async-start(), calls=%async_computation.3 | async-start | bytes 4718592 | tf_op jit(solution)/shard_map/reduce_scatter | solution.py:462
  199.0 50.4 %collective-permute-start = (bf16[768,512]{1,0:T(8,128)(2,1)}, bf16[768,512]{1,0:T(8,128)(2,1)}, u32[]{:S(2)}, u32[]{:S(2)}) collective-permute-start(bf16[768,512]{1,0:T(8,128)(2,1)} %get-tuple-element.60), channel_id=1, source_target_pairs={{0,8},{8,0},{16,24},{24,16},{1,9},{9,1},{17,25},{25,17},{2,10},{10... | collective-permute-start | bytes 2359304 | tf_op jit(solution)/shard_map/ppermute | solution.py:364
  208.4 48.7 %collective-permute-start.10 = (bf16[960,512]{1,0:T(8,128)(2,1)}, bf16[960,512]{1,0:T(8,128)(2,1)}, u32[]{:S(2)}, u32[]{:S(2)}) collective-permute-start(bf16[960,512]{1,0:T(8,128)(2,1)} %get-tuple-element.69), channel_id=1, source_target_pairs={{0,8},{8,0},{16,24},{24,16},{1,9},{9,1},{17,25},{25,17},{2,10},{10... | collective-permute-start | bytes 2949128 | tf_op jit(solution)/shard_map/ppermute | solution.py:364
  220.4 96.7 %collective-permute-start.20 = (bf16[1408,512]{1,0:T(8,128)(2,1)}, bf16[1408,512]{1,0:T(8,128)(2,1)S(1)}, u32[]{:S(2)}, u32[]{:S(2)}) collective-permute-start(bf16[1408,512]{1,0:T(8,128)(2,1)} %get-tuple-element.78), channel_id=1, source_target_pairs={{0,8},{8,0},{16,24},{24,16},{1,9},{9,1},{17,25},{25,17},{2,10},{10... | collective-permute-start | bytes 4325384 | tf_op jit(solution)/shard_map/ppermute | solution.py:364
  229.8 80.5 %collective-permute-start.15 = (bf16[960,512]{1,0:T(8,128)(2,1)}, bf16[960,512]{1,0:T(8,128)(2,1)S(1)}, u32[]{:S(2)}, u32[]{:S(2)}) collective-permute-start(bf16[960,512]{1,0:T(8,128)(2,1)} %get-tuple-element.73), channel_id=1, source_target_pairs={{0,16},{16,0},{8,24},{24,8},{1,17},{17,1},{9,25},{25,9},{2,18},{18... | collective-permute-start | bytes 2949128 | tf_op jit(solution)/shard_map/ppermute | solution.py:364
  242.6 85.3 %collective-permute-start.25 = (bf16[1408,512]{1,0:T(8,128)(2,1)}, bf16[1408,512]{1,0:T(8,128)(2,1)S(1)}, u32[]{:S(2)}, u32[]{:S(2)}) collective-permute-start(bf16[1408,512]{1,0:T(8,128)(2,1)} %get-tuple-element.82), channel_id=1, source_target_pairs={{0,16},{16,0},{8,24},{24,8},{1,17},{17,1},{9,25},{25,9},{2,18},{18... | collective-permute-start | bytes 4325384 | tf_op jit(solution)/shard_map/ppermute | solution.py:364
  249.4 53.1 %collective-permute-start.5 = (bf16[768,512]{1,0:T(8,128)(2,1)}, bf16[768,512]{1,0:T(8,128)(2,1)}, u32[]{:S(2)}, u32[]{:S(2)}) collective-permute-start(bf16[768,512]{1,0:T(8,128)(2,1)} %get-tuple-element.64), channel_id=1, source_target_pairs={{0,16},{16,0},{8,24},{24,8},{1,17},{17,1},{9,25},{25,9},{2,18},{18... | collective-permute-start | bytes 2359304 | tf_op jit(solution)/shard_map/ppermute | solution.py:364
  257.2 67.4 %collective-permute-start.1 = (bf16[768,256]{1,0:T(8,128)(2,1)}, bf16[768,256]{1,0:T(8,128)(2,1)}, u32[]{:S(2)}, u32[]{:S(2)}) collective-permute-start(bf16[768,256]{1,0:T(8,128)(2,1)} %get-tuple-element.62), channel_id=1, source_target_pairs={{0,16},{16,0},{8,24},{24,8},{1,17},{17,1},{9,25},{25,9},{2,18},{18... | collective-permute-start | bytes 1179656 | tf_op jit(solution)/shard_map/ppermute | solution.py:366
  302.6 32.9 %collective-permute-start.11 = (bf16[960,256]{1,0:T(8,128)(2,1)}, bf16[960,256]{1,0:T(8,128)(2,1)}, u32[]{:S(2)}, u32[]{:S(2)}) collective-permute-start(bf16[960,256]{1,0:T(8,128)(2,1)} %get-tuple-element.71), channel_id=1, source_target_pairs={{0,16},{16,0},{8,24},{24,8},{1,17},{17,1},{9,25},{25,9},{2,18},{18... | collective-permute-start | bytes 1474568 | tf_op jit(solution)/shard_map/ppermute | solution.py:366
  310.3 16.1 %collective-permute-start.6 = (bf16[768,256]{1,0:T(8,128)(2,1)}, bf16[768,256]{1,0:T(8,128)(2,1)}, u32[]{:S(2)}, u32[]{:S(2)}) collective-permute-start(bf16[768,256]{1,0:T(8,128)(2,1)} %get-tuple-element.66), channel_id=1, source_target_pairs={{0,8},{8,0},{16,24},{24,16},{1,9},{9,1},{17,25},{25,17},{2,10},{10... | collective-permute-start | bytes 1179656 | tf_op jit(solution)/shard_map/ppermute | solution.py:366
  317.1 20.7 %collective-permute-start.16 = (bf16[960,256]{1,0:T(8,128)(2,1)}, bf16[960,256]{1,0:T(8,128)(2,1)S(1)}, u32[]{:S(2)}, u32[]{:S(2)}) collective-permute-start(bf16[960,256]{1,0:T(8,128)(2,1)} %get-tuple-element.75), channel_id=1, source_target_pairs={{0,8},{8,0},{16,24},{24,16},{1,9},{9,1},{17,25},{25,17},{2,10},{10... | collective-permute-start | bytes 1474568 | tf_op jit(solution)/shard_map/ppermute | solution.py:366
  324.6 39.8 %collective-permute-start.21 = (bf16[1408,256]{1,0:T(8,128)(2,1)}, bf16[1408,256]{1,0:T(8,128)(2,1)}, u32[]{:S(2)}, u32[]{:S(2)}) collective-permute-start(bf16[1408,256]{1,0:T(8,128)(2,1)} %get-tuple-element.80), channel_id=1, source_target_pairs={{0,16},{16,0},{8,24},{24,8},{1,17},{17,1},{9,25},{25,9},{2,18},{18... | collective-permute-start | bytes 2162696 | tf_op jit(solution)/shard_map/ppermute | solution.py:366
  326.3 41.7 %copy-start.9 = (bf16[768,256]{1,0:T(8,128)(2,1)}, bf16[768,256]{1,0:T(8,128)(2,1)S(1)}, u32[]{:S(2)}) copy-start(bf16[768,256]{1,0:T(8,128)(2,1)S(1)} %add.226.refs_0_) | copy-start | bytes 1179652
  326.3 23.3 %collective-permute-start.2 = (bf16[768,256]{1,0:T(8,128)(2,1)S(1)}, bf16[768,256]{1,0:T(8,128)(2,1)}, u32[]{:S(2)}, u32[]{:S(2)}) collective-permute-start(bf16[768,256]{1,0:T(8,128)(2,1)S(1)} %add.226.refs_0_), channel_id=1, source_target_pairs={{0,16},{16,0},{8,24},{24,8},{1,17},{17,1},{9,25},{25,9},{2,18},{18... | collective-permute-start | bytes 1179656 | tf_op jit(solution)/shard_map/ppermute | solution.py:367
  327.9 22.3 %collective-permute-start.3 = (bf16[768,256]{1,0:T(8,128)(2,1)S(1)}, bf16[768,256]{1,0:T(8,128)(2,1)S(1)}, u32[]{:S(2)}, u32[]{:S(2)}) collective-permute-start(bf16[768,256]{1,0:T(8,128)(2,1)S(1)} %add.226.refs_0_), channel_id=1, source_target_pairs={{0,8},{8,0},{16,24},{24,16},{1,9},{9,1},{17,25},{25,17},{2,10},{10... | collective-permute-start | bytes 1179656 | tf_op jit(solution)/shard_map/ppermute | solution.py:371
  335.5 32.5 %copy-start.15 = (bf16[1408,256]{1,0:T(8,128)(2,1)S(1)}, bf16[1408,256]{1,0:T(8,128)(2,1)}, u32[]{:S(2)}) copy-start(bf16[1408,256]{1,0:T(8,128)(2,1)} %get-tuple-element.83) | copy-start | bytes 2162692
  335.5 30.4 %collective-permute-start.26 = (bf16[1408,256]{1,0:T(8,128)(2,1)}, bf16[1408,256]{1,0:T(8,128)(2,1)S(1)}, u32[]{:S(2)}, u32[]{:S(2)}) collective-permute-start(bf16[1408,256]{1,0:T(8,128)(2,1)} %get-tuple-element.84), channel_id=1, source_target_pairs={{0,8},{8,0},{16,24},{24,16},{1,9},{9,1},{17,25},{25,17},{2,10},{10... | collective-permute-start | bytes 2162696 | tf_op jit(solution)/shard_map/ppermute | solution.py:366
  337.8 26.0 %collective-permute-start.7 = (bf16[768,256]{1,0:T(8,128)(2,1)S(1)}, bf16[768,256]{1,0:T(8,128)(2,1)S(1)}, u32[]{:S(2)}, u32[]{:S(2)}) collective-permute-start(bf16[768,256]{1,0:T(8,128)(2,1)S(1)} %add.230.refs_4_), channel_id=1, source_target_pairs={{0,8},{8,0},{16,24},{24,16},{1,9},{9,1},{17,25},{25,17},{2,10},{10... | collective-permute-start | bytes 1179656 | tf_op jit(solution)/shard_map/ppermute | solution.py:367
  349.6 18.6 %collective-permute-start.8 = (bf16[768,256]{1,0:T(8,128)(2,1)S(1)}, bf16[768,256]{1,0:T(8,128)(2,1)S(1)}, u32[]{:S(2)}, u32[]{:S(2)}) collective-permute-start(bf16[768,256]{1,0:T(8,128)(2,1)S(1)} %add.230.refs_4_), channel_id=1, source_target_pairs={{0,16},{16,0},{8,24},{24,8},{1,17},{17,1},{9,25},{25,9},{2,18},{18... | collective-permute-start | bytes 1179656 | tf_op jit(solution)/shard_map/ppermute | solution.py:371
  350.2 22.1 %collective-permute-start.4 = (bf16[768,256]{1,0:T(8,128)(2,1)}, bf16[768,256]{1,0:T(8,128)(2,1)S(1)}, u32[]{:S(2)}, u32[]{:S(2)}) collective-permute-start(bf16[768,256]{1,0:T(8,128)(2,1)} %collective-permute-done.2.refs_1_), channel_id=1, source_target_pairs={{0,8},{8,0},{16,24},{24,16},{1,9},{9,1},{17,25},{25,17},{2,10},{10... | collective-permute-start | bytes 1179656 | tf_op jit(solution)/shard_map/ppermute | solution.py:372
  363.8 23.2 %collective-permute-start.12 = (bf16[960,256]{1,0:T(8,128)(2,1)S(1)}, bf16[960,256]{1,0:T(8,128)(2,1)S(1)}, u32[]{:S(2)}, u32[]{:S(2)}) collective-permute-start(bf16[960,256]{1,0:T(8,128)(2,1)S(1)} %add.232.refs_0_), channel_id=1, source_target_pairs={{0,16},{16,0},{8,24},{24,8},{1,17},{17,1},{9,25},{25,9},{2,18},{18... | collective-permute-start | bytes 1474568 | tf_op jit(solution)/shard_map/ppermute | solution.py:367
  364.4 22.0 %collective-permute-start.9 = (bf16[768,256]{1,0:T(8,128)(2,1)S(1)}, bf16[768,256]{1,0:T(8,128)(2,1)S(1)}, u32[]{:S(2)}, u32[]{:S(2)}) collective-permute-start(bf16[768,256]{1,0:T(8,128)(2,1)S(1)} %collective-permute-done.7.refs_5_), channel_id=1, source_target_pairs={{0,16},{16,0},{8,24},{24,8},{1,17},{17,1},{9,25},{25,9},{2,18},{18... | collective-permute-start | bytes 1179656 | tf_op jit(solution)/shard_map/ppermute | solution.py:372
  365.9 21.7 %collective-permute-start.13 = (bf16[960,256]{1,0:T(8,128)(2,1)S(1)}, bf16[960,256]{1,0:T(8,128)(2,1)S(1)}, u32[]{:S(2)}, u32[]{:S(2)}) collective-permute-start(bf16[960,256]{1,0:T(8,128)(2,1)S(1)} %add.232.refs_0_), channel_id=1, source_target_pairs={{0,8},{8,0},{16,24},{24,16},{1,9},{9,1},{17,25},{25,17},{2,10},{10... | collective-permute-start | bytes 1474568 | tf_op jit(solution)/shard_map/ppermute | solution.py:371
  368.0 60.0 %copy-start.2 = (bf16[1408,256]{1,0:T(8,128)(2,1)}, bf16[1408,256]{1,0:T(8,128)(2,1)S(1)}, u32[]{:S(2)}) copy-start(bf16[1408,256]{1,0:T(8,128)(2,1)S(1)} %add.236.refs_0_) | copy-start | bytes 2162692
  368.2 59.8 %copy-start.3 = (bf16[1408,256]{1,0:T(8,128)(2,1)}, bf16[1408,256]{1,0:T(8,128)(2,1)S(1)}, u32[]{:S(2)}) copy-start(bf16[1408,256]{1,0:T(8,128)(2,1)S(1)} %add.237.refs_4_) | copy-start | bytes 2162692
  368.2 51.1 %copy-start.25 = (bf16[768,256]{1,0:T(8,128)(2,1)}, bf16[768,256]{1,0:T(8,128)(2,1)S(1)}, u32[]{:S(2)}) copy-start(bf16[768,256]{1,0:T(8,128)(2,1)S(1)} %collective-permute-done.8.refs_6_) | copy-start | bytes 1179652
  368.2 41.8 %collective-permute-start.22 = (bf16[1408,256]{1,0:T(8,128)(2,1)S(1)}, bf16[1408,256]{1,0:T(8,128)(2,1)S(1)}, u32[]{:S(2)}, u32[]{:S(2)}) collective-permute-start(bf16[1408,256]{1,0:T(8,128)(2,1)S(1)} %add.236.refs_0_), channel_id=1, source_target_pairs={{0,16},{16,0},{8,24},{24,8},{1,17},{17,1},{9,25},{25,9},{2,18},{18... | collective-permute-start | bytes 2162696 | tf_op jit(solution)/shard_map/ppermute | solution.py:367
  372.3 47.1 %copy-start.26 = (bf16[768,256]{1,0:T(8,128)(2,1)}, bf16[768,256]{1,0:T(8,128)(2,1)S(1)}, u32[]{:S(2)}) copy-start(bf16[768,256]{1,0:T(8,128)(2,1)S(1)} %collective-permute-done.4.refs_3_) | copy-start | bytes 1179652
  372.3 39.2 %collective-permute-start.27 = (bf16[1408,256]{1,0:T(8,128)(2,1)S(1)}, bf16[1408,256]{1,0:T(8,128)(2,1)}, u32[]{:S(2)}, u32[]{:S(2)}) collective-permute-start(bf16[1408,256]{1,0:T(8,128)(2,1)S(1)} %add.237.refs_4_), channel_id=1, source_target_pairs={{0,8},{8,0},{16,24},{24,16},{1,9},{9,1},{17,25},{25,17},{2,10},{10... | collective-permute-start | bytes 2162696 | tf_op jit(solution)/shard_map/ppermute | solution.py:367
  373.0 55.0 %copy-start.8 = (bf16[960,256]{1,0:T(8,128)(2,1)}, bf16[960,256]{1,0:T(8,128)(2,1)S(1)}, u32[]{:S(2)}) copy-start(bf16[960,256]{1,0:T(8,128)(2,1)S(1)} %add.233.refs_4_) | copy-start | bytes 1474564
  386.4 32.9 %copy-start.27 = (bf16[768,256]{1,0:T(8,128)(2,1)}, bf16[768,256]{1,0:T(8,128)(2,1)S(1)}, u32[]{:S(2)}) copy-start(bf16[768,256]{1,0:T(8,128)(2,1)S(1)} %collective-permute-done.9.refs_7_) | copy-start | bytes 1179652
  386.4 22.5 %collective-permute-start.17 = (bf16[960,256]{1,0:T(8,128)(2,1)S(1)}, bf16[960,256]{1,0:T(8,128)(2,1)}, u32[]{:S(2)}, u32[]{:S(2)}) collective-permute-start(bf16[960,256]{1,0:T(8,128)(2,1)S(1)} %add.233.refs_4_), channel_id=1, source_target_pairs={{0,8},{8,0},{16,24},{24,16},{1,9},{9,1},{17,25},{25,17},{2,10},{10... | collective-permute-start | bytes 1474568 | tf_op jit(solution)/shard_map/ppermute | solution.py:367
  387.0 22.5 %collective-permute-start.18 = (bf16[960,256]{1,0:T(8,128)(2,1)S(1)}, bf16[960,256]{1,0:T(8,128)(2,1)S(1)}, u32[]{:S(2)}, u32[]{:S(2)}) collective-permute-start(bf16[960,256]{1,0:T(8,128)(2,1)S(1)} %add.233.refs_4_), channel_id=1, source_target_pairs={{0,16},{16,0},{8,24},{24,8},{1,17},{17,1},{9,25},{25,9},{2,18},{18... | collective-permute-start | bytes 1474568 | tf_op jit(solution)/shard_map/ppermute | solution.py:371
  387.6 31.7 %collective-permute-start.14 = (bf16[960,256]{1,0:T(8,128)(2,1)S(1)}, bf16[960,256]{1,0:T(8,128)(2,1)S(1)}, u32[]{:S(2)}, u32[]{:S(2)}) collective-permute-start(bf16[960,256]{1,0:T(8,128)(2,1)S(1)} %collective-permute-done.12.refs_1_), channel_id=1, source_target_pairs={{0,8},{8,0},{16,24},{24,16},{1,9},{9,1},{17,25},{25,17},{2,10},{10... | collective-permute-start | bytes 1474568 | tf_op jit(solution)/shard_map/ppermute | solution.py:372
  408.9 46.4 %collective-permute-start.23 = (bf16[1408,256]{1,0:T(8,128)(2,1)S(1)}, bf16[1408,256]{1,0:T(8,128)(2,1)}, u32[]{:S(2)}, u32[]{:S(2)}) collective-permute-start(bf16[1408,256]{1,0:T(8,128)(2,1)S(1)} %add.236.refs_0_), channel_id=1, source_target_pairs={{0,8},{8,0},{16,24},{24,16},{1,9},{9,1},{17,25},{25,17},{2,10},{10... | collective-permute-start | bytes 2162696 | tf_op jit(solution)/shard_map/ppermute | solution.py:371
  409.5 45.8 %collective-permute-start.28 = (bf16[1408,256]{1,0:T(8,128)(2,1)S(1)}, bf16[1408,256]{1,0:T(8,128)(2,1)}, u32[]{:S(2)}, u32[]{:S(2)}) collective-permute-start(bf16[1408,256]{1,0:T(8,128)(2,1)S(1)} %add.237.refs_4_), channel_id=1, source_target_pairs={{0,16},{16,0},{8,24},{24,8},{1,17},{17,1},{9,25},{25,9},{2,18},{18... | collective-permute-start | bytes 2162696 | tf_op jit(solution)/shard_map/ppermute | solution.py:371
  410.0 45.3 %collective-permute-start.24 = (bf16[1408,256]{1,0:T(8,128)(2,1)S(1)}, bf16[1408,256]{1,0:T(8,128)(2,1)}, u32[]{:S(2)}, u32[]{:S(2)}) collective-permute-start(bf16[1408,256]{1,0:T(8,128)(2,1)S(1)} %collective-permute-done.22.refs_1_), channel_id=1, source_target_pairs={{0,8},{8,0},{16,24},{24,16},{1,9},{9,1},{17,25},{25,17},{2,10},{10... | collective-permute-start | bytes 2162696 | tf_op jit(solution)/shard_map/ppermute | solution.py:372
  411.5 43.9 %collective-permute-start.29 = (bf16[1408,256]{1,0:T(8,128)(2,1)}, bf16[1408,256]{1,0:T(8,128)(2,1)}, u32[]{:S(2)}, u32[]{:S(2)}) collective-permute-start(bf16[1408,256]{1,0:T(8,128)(2,1)} %collective-permute-done.27.refs_5_), channel_id=1, source_target_pairs={{0,16},{16,0},{8,24},{24,8},{1,17},{17,1},{9,25},{25,9},{2,18},{18... | collective-permute-start | bytes 2162696 | tf_op jit(solution)/shard_map/ppermute | solution.py:372
  419.3 28.8 %collective-permute-start.19 = (bf16[960,256]{1,0:T(8,128)(2,1)}, bf16[960,256]{1,0:T(8,128)(2,1)}, u32[]{:S(2)}, u32[]{:S(2)}) collective-permute-start(bf16[960,256]{1,0:T(8,128)(2,1)} %collective-permute-done.17.refs_5_), channel_id=1, source_target_pairs={{0,16},{16,0},{8,24},{24,8},{1,17},{17,1},{9,25},{25,9},{2,18},{18... | collective-permute-start | bytes 1474568 | tf_op jit(solution)/shard_map/ppermute | solution.py:372
  455.3 51.5 %copy-start.36 = (pred[128]{0:T(512)(128)(4,1)S(1)}, pred[128]{0:T(512)(128)(4,1)}, u32[]{:S(2)}) copy-start(pred[128]{0:T(512)(128)(4,1)} %copy-done.35) | copy-start | bytes 388
  455.3 54.6 %copy-start.1 = (bf16[3,256,2048]{2,1,0:T(8,128)(2,1)S(1)}, bf16[3,256,2048]{2,1,0:T(8,128)(2,1)}, u32[]{:S(2)}) copy-start(bf16[3,256,2048]{2,1,0:T(8,128)(2,1)} %param.14) | copy-start | bytes 9437188
  (38 other events, 331.0 us)
Sparse Core Ops, SparseCore 0:
  14.3 49.8 all-gather.3
  66.4 27.8 all-gather.5
  95.8 28.5 all-gather.7
  181.1 49.5 reduce-scatter.4
  232.8 48.1 reduce-scatter.2

commit v3 on v2

v3 whole, which is shorter than its diff:
```python
import functools
import jax
import jax.numpy as jnp
from jax import lax
from jax.experimental import pallas as pl
from jax.experimental.pallas import tpu as pltpu
from jax.sharding import PartitionSpec as P

HEAD = 64
ROT = 16
MASKED = -1e30
LONG = 1000
EPSILON = 1e-05
ROOM = 16 * 2**20
IN_VMEM = pl.BlockSpec(memory_space=pltpu.VMEM)
IN_SMEM = pl.BlockSpec(memory_space=pltpu.SMEM)


def dot_rows(a, b):
    return lax.dot_general(a, b, (((1,), (0,)), ((), ())), preferred_element_type=jnp.float32)


def dot_lanes(a, b):
    return lax.dot_general(a, b, (((1,), (1,)), ((), ())), preferred_element_type=jnp.float32)


def dot_tall(a, b):
    return lax.dot_general(a, b, (((0,), (0,)), ((), ())), preferred_element_type=jnp.float32)


def turn(values, tables, sign):
    half = ROT // 2
    width = values.shape[1]
    tables = [jnp.concatenate([part] * (width // 128), axis=1) for part in tables]
    up = pltpu.roll(values, width - half, 1)
    down = pltpu.roll(values, half, 1)
    return values * tables[0] + sign * (up * tables[1] + down * tables[2])


def of_head(head, shape):
    return lax.broadcasted_iota(jnp.int32, shape, 1) // HEAD == head


def over_blocks(row_len, block, body):
    longest = row_len // 2
    blocks = row_len // block
    if blocks <= 8:
        for index in range(blocks):
            first = index * block
            start = max(0, first + block - (longest + block))
            body(first, start, first + block - start)
    else:
        size = longest + block

        def step(index, carry):
            first = pl.multiple_of(index * block, block)
            start = pl.multiple_of(jnp.maximum(first - longest, 0), block)
            body(first, start, size)
            return carry

        lax.fori_loop(0, blocks, step, 0)


def mask_of(seg_col, seg_row, first, start, block, size):
    rows = first + lax.broadcasted_iota(jnp.int32, (block, size), 0)
    keys = start + lax.broadcasted_iota(jnp.int32, (block, size), 1)
    same = seg_col[pl.ds(first, block), 0:1] == seg_row[0:1, pl.ds(start, size)]
    return jnp.where(same & (keys <= rows), 0.0, MASKED)


def forward_kernel(
    heads,
    hidden_in,
    projection,
    shift,
    tables,
    seg_col,
    seg_row,
    query,
    key,
    value,
    context,
    context_t,
    logsum,
):
    row_len, width = query.shape
    block = 256
    scale = HEAD ** (-0.5)
    for first in range(0, row_len, block):
        here = slice(first, first + block)
        lines = dot_lanes(hidden_in[here, :], projection[...]) + shift[...]
        turning = [tables[part, here, :] for part in range(3)]
        asked = turn(lines[:, 0:width], turning, 1.0).astype(jnp.bfloat16)
        query[here, :] = asked * jnp.bfloat16(scale)
        key[here, :] = turn(lines[:, width : 2 * width], turning, 1.0).astype(jnp.bfloat16)
        value[here, :] = lines[:, 2 * width : 3 * width].astype(jnp.bfloat16)

    def one_block(first, start, size):
        bias = mask_of(seg_col, seg_row, first, start, block, size)
        here = query[pl.ds(first, block), :]
        keys = key[pl.ds(start, size), :]
        values = value[pl.ds(start, size), :]
        total = jnp.zeros((block, width), jnp.float32)
        lane = lax.broadcasted_iota(jnp.int32, (block, 128), 1)
        sums = jnp.zeros((block, 128), jnp.float32)
        for head in range(heads):
            mine = of_head(head, (block, width))
            scores = dot_lanes(jnp.where(mine, here, jnp.bfloat16(0)), keys) + bias
            highest = jnp.max(scores, axis=1, keepdims=True)
            raised = jnp.exp(scores - highest)
            amount = jnp.sum(raised, axis=1, keepdims=True)
            weights = (raised * (1.0 / amount)).astype(jnp.bfloat16)
            total = jnp.where(mine, dot_rows(weights, values), total)
            sums = jnp.where(lane == head, highest + jnp.log(amount), sums)
        context[pl.ds(first, block), :] = total.astype(jnp.bfloat16)
        context_t[:, pl.ds(first, block)] = total.T.astype(jnp.bfloat16)
        logsum[pl.ds(first, block), :] = sums

    over_blocks(row_len, block, one_block)


def attend_forward(hidden_in, projection, shift, tables, seg_col, seg_row, heads):
    row_len, width = hidden_in.shape[0], projection.shape[0] // 3
    low = jax.ShapeDtypeStruct((row_len, width), jnp.bfloat16)
    return pl.pallas_call(
        functools.partial(forward_kernel, heads),
        in_specs=[IN_VMEM] * 6,
        out_shape=(
            low,
            low,
            low,
            low,
            jax.ShapeDtypeStruct((width, row_len), jnp.bfloat16),
            jax.ShapeDtypeStruct((row_len, 128), jnp.float32),
        ),
        compiler_params=pltpu.CompilerParams(vmem_limit_bytes=ROOM + 4096 * row_len),
        cost_estimate=busy(8.5),
        name="attend_forward",
    )(hidden_in, projection, shift, tables, seg_col, seg_row)


def backward_kernel(
    heads,
    query,
    key,
    value,
    grad_all,
    out_weight,
    logsum,
    tables,
    seg_col,
    seg_row,
    lines_low,
    lines_low_t,
    bias_grad,
    key_grad,
    value_grad,
):
    row_len, width = query.shape
    block = 256
    scale = HEAD ** (-0.5)
    key_grad[...] = jnp.zeros_like(key_grad)
    value_grad[...] = jnp.zeros_like(value_grad)
    bias_grad[...] = jnp.zeros_like(bias_grad)

    def put(part, first, grads):
        low = grads.astype(jnp.bfloat16)
        wide = low.astype(jnp.float32)
        columns = slice(part * width, (part + 1) * width)
        lines_low[pl.ds(first, block), columns] = low
        lines_low_t[columns, pl.ds(first, block)] = wide.T.astype(jnp.bfloat16)
        bias_grad[0:1, columns] += jnp.sum(wide, axis=0, keepdims=True)

    def one_block(first, start, size):
        bias = mask_of(seg_col, seg_row, first, start, block, size)
        here = query[pl.ds(first, block), :]
        grad_here = dot_lanes(grad_all[pl.ds(first, block), :], out_weight[...])
        grad_here = grad_here.astype(jnp.bfloat16)
        keys = key[pl.ds(start, size), :]
        values = value[pl.ds(start, size), :]
        sums = logsum[pl.ds(first, block), :]
        total = jnp.zeros((block, width), jnp.float32)
        for head in range(heads):
            mine = of_head(head, (block, width))
            asked = jnp.where(mine, here, jnp.bfloat16(0))
            pulled = jnp.where(mine, grad_here, jnp.bfloat16(0))
            scores = dot_lanes(asked, keys) + bias
            probs = jnp.exp(scores - sums[:, head : head + 1])
            prob_grad = dot_lanes(pulled, values)
            value_grad[pl.ds(start, size), :] += dot_tall(probs.astype(jnp.bfloat16), pulled)
            inner = jnp.sum(probs * prob_grad, axis=1, keepdims=True)
            score_low = (probs * (prob_grad - inner)).astype(jnp.bfloat16)
            total = jnp.where(mine, dot_rows(score_low, keys), total)
            key_grad[pl.ds(start, size), :] += dot_tall(score_low, asked)
        here_tables = [tables[part, pl.ds(first, block), :] for part in range(3)]
        put(0, first, turn(total * scale, here_tables, -1.0))

    over_blocks(row_len, block, one_block)
    for index in range(row_len // block):
        first = index * block
        here_tables = [tables[part, pl.ds(first, block), :] for part in range(3)]
        put(1, first, turn(key_grad[pl.ds(first, block), :], here_tables, -1.0))
        put(2, first, value_grad[pl.ds(first, block), :])


def attend_backward(
    query, key, value, grad_all, out_weight, logsum, tables, seg_col, seg_row, heads
):
    row_len, width = query.shape
    return pl.pallas_call(
        functools.partial(backward_kernel, heads),
        in_specs=[IN_VMEM] * 9,
        out_shape=(
            jax.ShapeDtypeStruct((row_len, 3 * width), jnp.bfloat16),
            jax.ShapeDtypeStruct((3 * width, row_len), jnp.bfloat16),
            jax.ShapeDtypeStruct((8, 3 * width), jnp.float32),
        ),
        scratch_shapes=[
            pltpu.VMEM((row_len, width), jnp.float32),
            pltpu.VMEM((row_len, width), jnp.float32),
        ],
        compiler_params=pltpu.CompilerParams(vmem_limit_bytes=ROOM + 4096 * row_len),
        cost_estimate=busy(13.3),
        name="attend_backward",
    )(query, key, value, grad_all, out_weight, logsum, tables, seg_col, seg_row)


def layout(doc_lengths, row_len):
    ends = jnp.cumsum(doc_lengths[0])
    starts = ends - doc_lengths[0]
    places = jnp.arange(row_len, dtype=jnp.int32)
    segment = jnp.sum((places[:, None] >= ends[None, :]).astype(jnp.int32), axis=1)
    chosen = segment[:, None] == jnp.arange(ends.shape[0], dtype=jnp.int32)[None, :]
    first = jnp.sum(jnp.where(chosen, starts[None, :], 0), axis=1)
    return segment, places - first, segment < ends.shape[0] - 1


def turns(position):
    half = ROT // 2
    lane = lax.broadcasted_iota(jnp.int32, (position.shape[0], 128), 1) % HEAD
    freq = 10000.0 ** (-((lane % half).astype(jnp.float32) * (2.0 / ROT)))
    angle = position.astype(jnp.float32)[:, None] * freq
    cosine, sine = jnp.cos(angle), jnp.sin(angle)
    return jnp.stack(
        [
            jnp.where(lane < ROT, cosine, 1.0),
            jnp.where(lane < half, -sine, 0.0),
            jnp.where((lane >= half) & (lane < ROT), sine, 0.0),
        ]
    )


def busy(time):
    return pl.CostEstimate(flops=int(time * 1.0 * 10**9), bytes_accessed=0, transcendentals=0)


def blocks_of(tokens):
    return min(512, tokens)


def gated_kernel(hidden_in, gate_weight, up_weight, gate, up, mixed, mixed_t):
    gate_here = dot_lanes(gate_weight[...], hidden_in[...])
    up_here = dot_lanes(up_weight[...], hidden_in[...])
    gate[...] = gate_here
    up[...] = up_here
    total = gate_here * jax.nn.sigmoid(gate_here) * up_here
    mixed_t[...] = total.astype(jnp.bfloat16)
    mixed[...] = total.T.astype(jnp.bfloat16)


def gated_forward(hidden_in, gate_weight, up_weight):
    (tokens, features), units = hidden_in.shape, gate_weight.shape[0]
    block = blocks_of(tokens)
    tall = pl.BlockSpec((units, block), lambda step: (0, step))
    flat = pl.BlockSpec((block, units), lambda step: (step, 0))
    return pl.pallas_call(
        gated_kernel,
        grid=(tokens // block,),
        in_specs=[pl.BlockSpec((block, features), lambda step: (step, 0)), IN_VMEM, IN_VMEM],
        out_specs=[tall, tall, flat, tall],
        out_shape=[
            jax.ShapeDtypeStruct((units, tokens), jnp.float32),
            jax.ShapeDtypeStruct((units, tokens), jnp.float32),
            jax.ShapeDtypeStruct((tokens, units), jnp.bfloat16),
            jax.ShapeDtypeStruct((units, tokens), jnp.bfloat16),
        ],
        compiler_params=pltpu.CompilerParams(vmem_limit_bytes=ROOM),
        cost_estimate=busy(7.5),
        name="gated_forward",
    )(hidden_in, gate_weight, up_weight)


def gated_back_kernel(
    grad_all, down_weight, gate, up, gate_low, gate_low_t, up_low, up_low_t
):
    mixed_grad = dot_lanes(down_weight[...], grad_all[...])
    gate_here = gate[...]
    sigmoid = jax.nn.sigmoid(gate_here)
    pulled = mixed_grad * sigmoid
    gate_grad = pulled * up[...] * (1.0 + gate_here * (1.0 - sigmoid))
    up_grad = pulled * gate_here
    gate_low_t[...] = gate_grad.astype(jnp.bfloat16)
    up_low_t[...] = up_grad.astype(jnp.bfloat16)
    gate_low[...] = gate_grad.T.astype(jnp.bfloat16)
    up_low[...] = up_grad.T.astype(jnp.bfloat16)


def gated_backward(grad_all, down_weight, gate, up):
    (tokens, features), units = grad_all.shape, down_weight.shape[0]
    block = blocks_of(tokens)
    tall = pl.BlockSpec((units, block), lambda step: (0, step))
    flat = pl.BlockSpec((block, units), lambda step: (step, 0))
    wide = jax.ShapeDtypeStruct((tokens, units), jnp.bfloat16)
    long = jax.ShapeDtypeStruct((units, tokens), jnp.bfloat16)
    return pl.pallas_call(
        gated_back_kernel,
        grid=(tokens // block,),
        in_specs=[pl.BlockSpec((block, features), lambda step: (step, 0)), IN_VMEM, tall, tall],
        out_specs=[flat, tall, flat, tall],
        out_shape=[wide, long, wide, long],
        compiler_params=pltpu.CompilerParams(vmem_limit_bytes=ROOM),
        cost_estimate=busy(5.4),
        name="gated_backward",
    )(grad_all, down_weight, gate, up)


def merge_kernel(count, *refs):
    total = dot_rows(refs[0][...], refs[count][...])
    for index in range(1, count):
        total = total + dot_rows(refs[index][...], refs[count + index][...])
    refs[2 * count][...] = total.astype(jnp.bfloat16)


def merge(lhs, weights):
    tokens, features, count = lhs[0].shape[0], weights[0].shape[1], len(lhs)
    block = min(256, tokens)
    return pl.pallas_call(
        functools.partial(merge_kernel, count),
        grid=(tokens // block,),
        in_specs=[
            *(pl.BlockSpec((block, part.shape[1]), lambda step: (step, 0)) for part in lhs),
            *([IN_VMEM] * count),
        ],
        out_specs=pl.BlockSpec((block, features), lambda step: (step, 0)),
        out_shape=jax.ShapeDtypeStruct((tokens, features), jnp.bfloat16),
        compiler_params=pltpu.CompilerParams(vmem_limit_bytes=ROOM),
        cost_estimate=busy(8),
        name="merge",
    )(*lhs, *weights)


def stacked(lhs, which, rhs, first, wide, keep):
    row = 0
    blocks = [part[:, pl.ds(pl.multiple_of(at, 128), wide)] for part, at in zip(rhs, first)]
    for part, index in zip(lhs, which):
        keep(row, part.shape[0], dot_rows(part[...], blocks[index]))
        row += part.shape[0]


def send_kernel(which, wide, order, *refs):
    count = len(which)
    lhs, rhs, outs = refs[:count], refs[count:-2], refs[-2:]
    for half, out in enumerate(outs):

        def keep(row, rows, term, out=out):
            out[row : row + rows, :] = term.astype(jnp.bfloat16)

        first = [order[half, index] for index in range(len(rhs))]
        stacked(lhs, which, rhs, first, wide, keep)


def join_kernel(which, wide, order, *refs):
    count = len(which)
    lhs, rhs, came = refs[:count], refs[count:-7], refs[-7:-5]
    outs, total = refs[-5:-1], refs[-1]
    narrow = wide // 2
    for half in range(2):

        def keep(row, rows, term, half=half):
            there = came[half][row : row + rows, :].astype(jnp.float32)
            total[row : row + rows, :] = (term + there).astype(jnp.bfloat16)

        first = [order[half, index] for index in range(len(rhs))]
        stacked(lhs, which, rhs, first, wide, keep)
        bit = order[2, half]
        outs[2 * half][...] = total[:, pl.ds(pl.multiple_of((1 - bit) * narrow, narrow), narrow)]
        outs[2 * half + 1][...] = total[:, pl.ds(pl.multiple_of(bit * narrow, narrow), narrow)]


def place_kernel(order, *refs):
    pieces, outs = refs[:6], refs[6:]
    rows = pieces[0].shape[0]
    step = pl.program_id(0)
    for index in range(8):
        piece, start = pieces[min(index, 4 + index % 2)], rows * (index // 6)

        @pl.when(step == index)
        def _(piece=piece, start=start):
            first = start
            for out in outs:
                size = out.shape[0]
                out[...] = piece[first : first + size, :].astype(jnp.float32)
                first += size


def place(pieces, order, sizes, features):
    rows, narrow = pieces[0].shape
    return pl.pallas_call(
        place_kernel,
        grid_spec=pltpu.PrefetchScalarGridSpec(
            num_scalar_prefetch=1,
            grid=(8,),
            in_specs=[IN_VMEM] * len(pieces),
            out_specs=[
                pl.BlockSpec((size, narrow), lambda step, order: (0, order[step]))
                for size in sizes
            ],
        ),
        out_shape=[jax.ShapeDtypeStruct((size, features), jnp.float32) for size in sizes],
        compiler_params=pltpu.CompilerParams(vmem_limit_bytes=ROOM),
        cost_estimate=busy(6.5),
        name="place",
    )(jnp.stack(order).astype(jnp.int32), *pieces)


NEAR = [(0, 1), (1, 0), (2, 3), (3, 2)]
FAR = [(0, 2), (2, 0), (1, 3), (3, 1)]
PATHS = ((NEAR, FAR), (FAR, NEAR))


def after(value, *others):
    return lax.optimization_barrier((value, others))[0]


class Sum:
    def __init__(self, lhs, which, rhs, starts, columns, time=0):
        row = lax.axis_index("rows")
        near, far = row % 2, row // 2
        self.bits = ((near, far), (far, near))
        self.lhs, self.which, self.rhs, self.starts = lhs, which, rhs, starts
        self.narrow = columns // 8
        self.time = time
        self.rows = sum(part.shape[0] for part in lhs)

    def first(self, half, bit):
        return [start + self.narrow * (4 * half + 2 * bit) for start in self.starts]

    def piece(self, wide):
        return jax.ShapeDtypeStruct((self.rows, wide), jnp.bfloat16)

    def send(self, *earlier):
        order = jnp.array([self.first(half, 1 - self.bits[half][0]) for half in range(2)])
        wide = 2 * self.narrow
        head = after(self.lhs[0], *earlier)
        sent = pl.pallas_call(
            functools.partial(send_kernel, self.which, wide),
            in_specs=[IN_SMEM] + [IN_VMEM] * (len(self.lhs) + len(self.rhs)),
            out_shape=[self.piece(wide)] * 2,
            compiler_params=pltpu.CompilerParams(vmem_limit_bytes=ROOM + 2048 * self.lhs[0].shape[1]),
            cost_estimate=busy(self.rows / 256),
            name="send_terms",
        )(order.astype(jnp.int32), head, *self.lhs[1:], *self.rhs)
        self.came = [lax.ppermute(sent[half], "rows", PATHS[half][0]) for half in range(2)]
        return sent[0]

    def join(self, *earlier):
        wide = 2 * self.narrow
        order = [[*self.first(half, self.bits[half][0]), 0][:2] for half in range(2)]
        order.append([self.bits[0][1], self.bits[1][1]])
        head = after(self.lhs[0], *earlier)
        outs = pl.pallas_call(
            functools.partial(join_kernel, self.which, wide),
            in_specs=[IN_SMEM] + [IN_VMEM] * (len(self.lhs) + len(self.rhs) + 2),
            out_shape=[self.piece(self.narrow)] * 4,
            scratch_shapes=[pltpu.VMEM((self.rows, wide), jnp.bfloat16)],
            compiler_params=pltpu.CompilerParams(vmem_limit_bytes=ROOM + 2048 * self.lhs[0].shape[1]),
            cost_estimate=busy(self.time if self.time else self.rows / 256),
            name="join_terms",
        )(jnp.array(order).astype(jnp.int32), head, *self.lhs[1:], *self.rhs, *self.came)
        self.mine = [outs[1], outs[3]]
        self.came = [lax.ppermute(outs[2 * half], "rows", PATHS[half][1]) for half in range(2)]
        return outs[0]

    def total(self, *earlier):
        mine = lax.optimization_barrier((*self.mine, *earlier))[:2]
        self.mine = [mine[half] + self.came[half] for half in range(2)]
        self.across = [lax.ppermute(self.mine[half], "rows", PATHS[half][1]) for half in range(2)]
        return self.mine

    def share(self, *earlier):
        mine = lax.optimization_barrier((*self.mine, *earlier))[:2]
        both = [jnp.concatenate([mine[half], self.across[half]]) for half in range(2)]
        self.last = [lax.ppermute(both[half], "rows", PATHS[half][0]) for half in range(2)]
        return both

    def place(self, features, *earlier):
        order = []
        for first, second in ((0, 0), (0, 1), (1, 0), (1, 1)):
            for half in range(2):
                a, b = self.bits[half]
                order.append(4 * half + 2 * jnp.abs(a - first) + jnp.abs(b - second))
        mine = lax.optimization_barrier((*self.mine, *earlier))[:2]
        sizes = [part.shape[0] for part in self.lhs]
        return place([*mine, *self.across, *self.last], order, sizes, features)


def sum_everywhere(values, axis):
    size, step = lax.axis_size(axis), 1
    while step < size:
        values = values + lax.ppermute(values, axis, [(i, i ^ step) for i in range(size)])
        step *= 2
    return values


def standardize(values):
    centre = jnp.mean(values, axis=1, keepdims=True)
    centred = values - centre
    spread = jnp.mean(centred * centred, axis=1, keepdims=True)
    inverse = lax.rsqrt(spread + EPSILON)
    return (centred * inverse, inverse)


def widen(weight, width):
    return jnp.pad(weight, ((0, 0), (0, width - weight.shape[1]), (0, 0)))


def per_device(
    block_input,
    norm_gain,
    norm_bias,
    qkv_weight,
    qkv_bias,
    out_weight,
    gate_weight,
    up_weight,
    down_weight,
    cotangent,
    doc_lengths,
):
    shard, features = block_input.shape
    group = lax.axis_size("tp")
    tokens = shard * group
    width = qkv_weight.shape[1]
    heads = width // HEAD
    padded = max(width, 128)
    me = lax.axis_index("tp")
    segment, position, live = layout(doc_lengths, tokens)
    live_mine = lax.dynamic_slice_in_dim(live, me * shard, shard)[:, None]
    input_wide = block_input.astype(jnp.float32)
    gain = norm_gain.astype(jnp.float32)
    shift = norm_bias.astype(jnp.float32)
    normed, inverse = standardize(input_wide)
    normed_low = (normed * gain + shift).astype(jnp.bfloat16)
    hidden_in = lax.all_gather(normed_low, "tp", axis=0, tiled=True)
    grad_mine = jnp.where(live_mine, cotangent, jnp.zeros_like(cotangent))
    grad_all = lax.all_gather(after(grad_mine, hidden_in), "tp", axis=0, tiled=True)
    tables = turns(position)
    seg_col = jnp.broadcast_to(segment[:, None], (tokens, 128))
    seg_row = jnp.broadcast_to(segment[None, :], (8, tokens))

    projection = widen(qkv_weight, padded).reshape(3 * padded, features)
    shift_lines = widen(qkv_bias[..., None], padded).reshape(1, 3 * padded).astype(jnp.float32)
    out_wide = widen(out_weight[None], padded)[0]
    gate, up, mixed, mixed_t = gated_forward(hidden_in, gate_weight, up_weight)
    query, key, value, context, context_t, logsum = attend_forward(
        after(hidden_in, mixed), projection, shift_lines, tables, seg_col, seg_row, heads
    )
    merged = merge([context, mixed], [out_wide, down_weight])
    down_sum = Sum([mixed_t], [0], [grad_all], [0], features)
    order = down_sum.send(merged)
    gate_low, gate_low_t, up_low, up_low_t = gated_backward(
        after(grad_all, order), down_weight, gate, up
    )
    inner_sum = Sum([gate_low_t, up_low_t], [0, 0], [hidden_in], [0], features, LONG)
    order = inner_sum.send()
    order = down_sum.join(order)
    lines_low, lines_low_t, bias_grad = attend_backward(
        query,
        key,
        value,
        after(grad_all, order),
        out_wide,
        logsum,
        tables,
        seg_col,
        seg_row,
        heads,
    )
    bias_grad = bias_grad[0].reshape(3, padded)[:, :width]
    outer_sum = Sum([lines_low_t, context_t], [0, 1], [hidden_in, grad_all], [0, 0], features, LONG)
    term = merge([gate_low, up_low, lines_low], [gate_weight, up_weight, projection])
    order = down_sum.total(term)
    order = inner_sum.join(order)
    order = down_sum.share(order)
    order = outer_sum.send(order)
    (down_grad,) = down_sum.place(features, order)
    order = inner_sum.total(down_grad)
    order = outer_sum.join(order)
    normed_grad = lax.psum_scatter(term, "tp", scatter_dimension=0, tiled=True)
    normed_grad = after(normed_grad, order).astype(jnp.float32)
    sums = jnp.concatenate([jnp.sum(normed_grad * normed, axis=0), jnp.sum(normed_grad, axis=0)])
    sums = sum_everywhere(sums, "tp")
    order = inner_sum.share(sums)
    order = outer_sum.total(order)
    sums = after(jnp.concatenate([sums, bias_grad.reshape(-1)]), order)
    sums = sum_everywhere(sums, "rows")
    order = outer_sum.share(sums)
    merged = lax.psum_scatter(merged, "tp", scatter_dimension=0, tiled=True)
    merged = merged.astype(jnp.float32)
    output = (input_wide + jnp.where(live_mine, merged, 0.0)).astype(jnp.bfloat16)
    scaled = normed_grad * gain
    input_grad = inverse * (
        scaled
        - jnp.mean(scaled, axis=1, keepdims=True)
        - normed * jnp.mean(scaled * normed, axis=1, keepdims=True)
    )
    input_grad = input_grad + cotangent.astype(jnp.float32)
    gate_grad, up_grad = inner_sum.place(features, order)
    qkv_grad, out_grad = outer_sum.place(features, gate_grad)
    return (
        output,
        input_grad,
        sums[:features],
        sums[features : 2 * features],
        qkv_grad.reshape(3, padded, features)[:, :width],
        sums[2 * features :].reshape(3, width),
        out_grad[:width],
        gate_grad,
        up_grad,
        down_grad,
    )


def solution(mesh):
    placed = (
        P(("rows", "tp"), None),
        P(),
        P(),
        P(None, "tp", None),
        P(None, "tp"),
        P("tp", None),
        P("tp", None),
        P("tp", None),
        P("tp", None),
        P(("rows", "tp"), None),
        P("rows", None),
    )
    return jax.shard_map(
        per_device,
        mesh=mesh,
        in_specs=placed,
        out_specs=(
            P(("rows", "tp"), None),
            P(("rows", "tp"), None),
            P(),
            P(),
            P(None, "tp", None),
            P(None, "tp"),
            P("tp", None),
            P("tp", None),
            P("tp", None),
            P("tp", None),
        ),
        check_vma=False,
    )
```

time: 521 us -> 387 us (0.74)
  matrix products: 62.1 us -> 0 us
  Pallas kernels: 136 us -> 95.5 us
  blocking collectives: 39.6 us -> 0 us
  local copies, waits for them, and re-layouts: 22.2 us -> 47.5 us
  waiting for transfers between devices: 186 us -> 175 us
    dot_general x12 -> x0, matrix products: 62.1 us -> none  [the longest x9 44 us: product(): return jnp.dot(a, b, preferred_element_type=jnp.float32)]
    pallas_call x17 -> x15, Pallas kernels: 136 us -> 95.5 us  [the longest x3 20.9 us: place(): pl.pallas_call(place_kernel, grid_spec=pltpu.PrefetchScalarGridSpec(num_s...]
    psum x1 -> x0, blocking collectives: 39.6 us -> none  [per_device(): small = lax.psum(small, ('rows', 'tp'))]
    unnamed x102 -> x153, local copies, waits for them, and re-layouts: 3.94 us -> 39.5 us
    another operation x8 -> x1, local copies, waits for them, and re-layouts: 12.5 us -> 0.08 us  [place(): jnp.stack(order).astype(jnp.int32)]
    ppermute x30 -> x29, waiting for transfers between devices: 124 us -> 115 us  [the longest x5 43.2 us: sum_everywhere(): lax.ppermute(values, axis, [(i, i ^ step) for i in range(size)])]
    concatenate x2 -> x6, local copies, waits for them, and re-layouts: 0.15 us -> 6.39 us  [share(): jnp.concatenate([mine[half], self.across[half]])]
    another operation x5 -> x2, other arithmetic: 6.51 us -> 0.29 us  [the longest x1 3.88 us: turns(): return jnp.stack([jnp.tile(part, (1, width // HEAD)) for part in parts])]
  transfers between devices with their start and end apart: 35 -> 33, of which waited for: 10 -> 16; matrix products, arithmetic and copies ran while one was open for 13% -> 8% of each run, Pallas kernels for 23% -> 23%
where the time goes in v3:
time: 387 us; the launch traced here: 383 us
  waiting for transfers between devices  175 us (45%)
  Pallas kernels  95.5 us (25%)
  local copies, waits for them, and re-layouts  47.5 us (12%)
  starting transfers between devices  28.1 us (7%)
  other arithmetic  22 us (6%)
  between operations  14.7 us (4%)
    all_gather x1, waiting for transfers between devices, per_device(): hidden_in = lax.all_gather(normed_low, 'tp', axis=0, tiled=True)  48.7 us
    ppermute x5, waiting for transfers between devices, sum_everywhere(): lax.ppermute(values, axis, [(i, i ^ step) for i in range(size)])  43.2 us
    ppermute x6, waiting for transfers between devices, join(): lax.ppermute(outs[2 * half], 'rows', PATHS[half][1])  39.6 us
    unnamed x153, local copies, waits for them, and re-layouts  39.5 us
    pallas_call x3, Pallas kernels, place(): pl.pallas_call(place_kernel, grid_spec=pltpu.PrefetchScalarGridSpec(num_s...  20.9 us
    ppermute x6, waiting for transfers between devices, share(): lax.ppermute(both[half], 'rows', PATHS[half][0])  16.1 us
    pallas_call x2, Pallas kernels, merge(): pl.pallas_call(functools.partial(merge_kernel, count), grid=(tokens // bl...  15.9 us
    pallas_call x1, Pallas kernels, attend_backward(): pl.pallas_call(functools.partial(backward_kernel, heads), in_specs=[IN_VM...  13.2 us
  transfers between devices with their start and end apart: 33, of which 16 were waited for; matrix products, arithmetic and copies ran while one was open for 8% of the time, Pallas kernels for 23%

profile of v3, /device:TPU:0, one launch (start us, length us, event | category | flops | bytes accessed | tf_op | source)
XLA Modules:
  0.0 382.8 jit_solution(17103465291773008509)
XLA Ops:
  11.3 2.2 fusion.8
  14.9 48.7 %all-gather.3.cloned.1.call-done.hidden_in.refs_2_ = bf16[1024,2048]{1,0:T(8,128)(2,1)} async-done(((bf16[128,2048]{1,0:T(8,128)(2,1)}), bf16[1024,2048]{1,0:T(8,128)(2,1)}) %all-gather.3.cloned.1.call-update) | async-done | bytes 4194320 | tf_op jit(solution)/shard_map/all_gather | solution.py:554
  64.1 2.0 fusion.17
  66.3 1.8 copy-done.28
  68.1 1.8 copy-done.30
  70.0 7.4 %gated_forward.1 = (f32[704,1024]{1,0:T(8,128)S(1)}, f32[704,1024]{1,0:T(8,128)S(1)}, bf16[1024,704]{1,0:T(8,128)(2,1)S(1)}, bf16[704,1024]{1,0:T(8,128)(2,1)S(1)}) custom-call(bf16[1024,2048]{1,0:T(8,128)(2,1)S(1)} %copy-done.16, bf16[704,2048]{1,0:T(8,128)(2,1)S(1)} %copy-done.28, bf16[704,2048]{1,0:T(8,128)(2,1)S(1)} %copy-done.30), custom_call_target="tpu_custom_call" | custom-call | flops 7500000256 | tf_op jit(solution)/shard_map/gated_forward/pallas_call | solution.py:276
  78.9 1.6 copy-done.45
  80.7 8.7 %attend_forward.1 = (bf16[1024,256]{1,0:T(8,128)(2,1)S(1)}, bf16[1024,256]{1,0:T(8,128)(2,1)S(1)}, bf16[1024,256]{1,0:T(8,128)(2,1)S(1)}, bf16[1024,256]{1,0:T(8...) custom-call(bf16[1024,2048]{1,0:T(8,128)(2,1)S(1)} %copy-done.16, bf16[768,2048]{1,0:T(8,128)(2,1)S(1)} %bitcast.45, ...), custom_call_target="tpu_custom_call" | custom-call | flops 8499999744 | tf_op jit(solution)/shard_map/attend_forward/pallas_call | solution.py:125
  93.4 5.5 %merge.2 = bf16[1024,2048]{1,0:T(8,128)(2,1)S(1)} custom-call(bf16[1024,256]{1,0:T(8,128)(2,1)S(1)} %get-tuple-element.80.refs_0_, bf16[1024,704]{1,0:T(8,128)(2,1)S(1)} %get-tuple-element.78.refs_1_, bf16[256,2048]{1,0:T(8,128)(2,1)S(1)} %copy-done.32, bf16[704,2048]{1,0:T(8,128)(2,1)S(1)} %copy-done.26), custom_call_target="tpu_custom_call" | custom-call | flops 8000000000 | tf_op jit(solution)/shard_map/merge/pallas_call | solution.py:337
  98.9 2.0 copy-done
  100.9 10.7 %all-gather.5.cloned.1.call-done.refs_1_.grad_all.refs_3_ = bf16[1024,2048]{1,0:T(8,128)(2,1)} async-done(((bf16[128,2048]{1,0:T(8,128)(2,1)}), bf16[1024,2048]{1,0:T(8,128)(2,1)}) %all-gather.5.cloned.1.call-update) | async-done | bytes 4194320 | tf_op jit(solution)/shard_map/all_gather | solution.py:556
  111.6 2.2 copy-done.20
  115.2 2.2 send_terms.3
  120.4 1.8 copy-done.46
  122.2 5.4 %gated_backward.1 = (bf16[1024,704]{1,0:T(8,128)(2,1)S(1)}, bf16[704,1024]{1,0:T(8,128)(2,1)S(1)}, bf16[1024,704]{1,0:T(8,128)(2,1)S(1)}, bf16[704,1024]{1,0:T(8,128)(2,1)S(1)}) custom-call(bf16[1024,2048]{1,0:T(8,128)(2,1)S(1)} %copy-done.21, bf16[704,2048]{1,0:T(8,128)(2,1)S(1)} %copy-done.27, f32[704,1024]{1,0:T(8,128)S(1)} %copy-done.44, ...), custom_call_target="tpu_custom_call" | custom-call | flops 5400000000 | tf_op jit(solution)/shard_map/gated_backward/pallas_call | solution.py:315
  127.6 5.1 %send_terms.4 = (bf16[1408,512]{1,0:T(8,128)(2,1)}, bf16[1408,512]{1,0:T(8,128)(2,1)}) custom-call(s32[2,1]{1,0:T(2,128)S(1)} %pad_add_fusion.2.order, bf16[704,1024]{1,0:T(8,128)(2,1)S(1)} %get-tuple-element.108.refs_0_, bf16[704,1024]{1,0:T(8,128)(2,1)S(1)} %get-tuple-element.94.refs_1_, bf16[1024,2048]{1,0:T(8,128)(2,1)S(1)} %copy-done.17), custom_call_target="tpu_custom_call" | custom-call | flops 5500000256 | tf_op jit(solution)/shard_map/send_terms/pallas_call | solution.py:455
  134.4 3.5 collective-permute-done.1.refs_3_
  138.0 3.0 join_terms.3
  143.0 13.2 %attend_backward.1 = (bf16[1024,768]{1,0:T(8,128)(2,1)S(1)}, bf16[768,1024]{1,0:T(8,128)(2,1)S(1)}, f32[8,768]{1,0:T(8,128)S(1)}) custom-call(bf16[1024,256]{1,0:T(8,128)(2,1)S(1)} %copy-done.55, bf16[1024,256]{1,0:T(8,128)(2,1)S(1)} %copy-done.57, bf16[1024,256]{1,0:T(8,128)(2,1)S(1)} %copy-done.59, bf16[1024,2048]{1,0:T(8,128)(2,1)S(1)} %copy-done.21, ...), custom_call_target="tpu_custom_call" | custom-call | flops 13299999744 | tf_op jit(solution)/shard_map/attend_backward/pallas_call | solution.py:210
  157.4 10.4 %merge.3 = bf16[1024,2048]{1,0:T(8,128)(2,1)S(1)} custom-call(bf16[1024,704]{1,0:T(8,128)(2,1)S(1)} %get-tuple-element.88.refs_0_, bf16[1024,704]{1,0:T(8,128)(2,1)S(1)} %get-tuple-element.89.refs_1_, bf16[1024,768]{1,0:T(8,128)(2,1)S(1)} %get-tuple-element.101.refs_2_, bf16[704,2048]{1,0:T(8,128)(2,1)S(1)} %copy-done.29, bf16[704,2048]{1,0:T(8,128)(2,1)S(1)} %copy-done.31, ...), custom_call_target="tpu_custom_call" | custom-call | flops 8000000000 | tf_op jit(solution)/shard_map/merge/pallas_call | solution.py:337
  167.8 2.0 copy-done.1
  169.9 4.5 %collective-permute-done.3 = bf16[704,256]{1,0:T(8,128)(2,1)} collective-permute-done((bf16[704,256]{1,0:T(8,128)(2,1)}, bf16[704,256]{1,0:T(8,128)(2,1)}, u32[]{:S(2)}, u32[]{:S(2)}) %collective-permute-start.3) | collective-permute-done | bytes 360480 | tf_op jit(solution)/shard_map/ppermute | solution.py:481
  174.5 1.8 add.186.refs_1_
  177.8 1.8 add.185.refs_0_
  181.0 2.2 copy-done.18
  184.7 6.1 %join_terms.4 = (bf16[1408,256]{1,0:T(8,128)(2,1)}, bf16[1408,256]{1,0:T(8,128)(2,1)S(1)}, bf16[1408,256]{1,0:T(8,128)(2,1)}, bf16[1408,256]{1,0:T(8,128)(2,1)S(1)}) custom-call(s32[3,2]{1,0:T(4,128)S(1)} %get-tuple-element.158.order, bf16[704,1024]{1,0:T(8,128)(2,1)S(1)} %copy-done.48, bf16[704,1024]{1,0:T(8,128)(2,1)S(1)} %copy-done.50, ...), custom_call_target="tpu_custom_call" | custom-call | flops 999999995904 | tf_op jit(solution)/shard_map/join_terms/pallas_call | solution.py:471
  193.6 1.7 constant_dynamic-update-slice_fusion.1
  195.3 1.8 constant_dynamic-update-slice_fusion
  197.6 2.2 copy-done.22
  199.8 3.9 %send_terms.5 = (bf16[1024,512]{1,0:T(8,128)(2,1)}, bf16[1024,512]{1,0:T(8,128)(2,1)}) custom-call(s32[2,2]{1,0:T(2,128)S(1)} %pad_add_fusion.3.order, bf16[768,1024]{1,0:T(8,128)(2,1)S(1)} %copy-done.41, bf16[256,1024]{1,0:T(8,128)(2,1)S(1)} %copy-done.52, bf16[1024,2048]{1,0:T(8,128)(2,1)S(1)} %copy-done.18, bf16[1024,2048]{1,0:T(8,128)(2,1)S(1)} %copy-done.22), custom_call_target="tpu_custom_call" | custom-call | flops 4000000000 | tf_op jit(solution)/shard_map/send_terms/pallas_call | solution.py:455
  207.3 4.8 %collective-permute-done.9.refs_5_ = bf16[1408,256]{1,0:T(8,128)(2,1)S(1)} collective-permute-done((bf16[1408,256]{1,0:T(8,128)(2,1)S(1)}, bf16[1408,256]{1,0:T(8,128)(2,1)S(1)}, u32[]{:S(2)}, u32[]{:S(2)}) %collective-permute-start.9) | collective-permute-done | bytes 720928 | tf_op jit(solution)/shard_map/ppermute | solution.py:493
  213.6 2.9 collective-permute-done.8.refs_4_
  217.6 6.6 %place.3 = f32[704,2048]{1,0:T(8,128)} custom-call(s32[8]{0:T(128)S(1)} %stack.29.order, bf16[704,256]{1,0:T(8,128)(2,1)} %add.185.refs_0_, bf16[704,256]{1,0:T(8,128)(2,1)} %add.186.refs_1_, bf16[704,256]{1,0:T(8,128)(2,1)} %collective-permute-done.6.refs_2_, bf16[704,256]{1,0:T(8,128)(2,1)} %collective-permute-done.7.refs_3_, ...), custom_call_target="tpu_custom_call" | custom-call | flops 6499999744 | tf_op jit(solution)/shard_map/place/pallas_call | solution.py:408
  224.2 23.6 %collective-permute-done.10 = bf16[1408,256]{1,0:T(8,128)(2,1)S(1)} collective-permute-done((bf16[1408,256]{1,0:T(8,128)(2,1)}, bf16[1408,256]{1,0:T(8,128)(2,1)S(1)}, u32[]{:S(2)}, u32[]{:S(2)}) %collective-permute-start.10) | collective-permute-done | bytes 720928 | tf_op jit(solution)/shard_map/ppermute | solution.py:481
  248.9 3.0 collective-permute-done.11
  252.0 2.2 add.198.refs_1_
  254.3 3.8 join_terms.5
  260.5 1.7 fusion.15
  263.9 3.8 collective-permute-done.15
  274.1 7.2 %collective-permute-done.17.refs_2_ = bf16[1408,256]{1,0:T(8,128)(2,1)S(1)} collective-permute-done((bf16[1408,256]{1,0:T(8,128)(2,1)S(1)}, bf16[1408,256]{1,0:T(8,128)(2,1)S(1)}, u32[]{:S(2)}, u32[]{:S(2)}) %collective-permute-start.17) | collective-permute-done | bytes 720928 | tf_op jit(solution)/shard_map/ppermute | solution.py:487
  282.2 5.8 %collective-permute-done.18.refs_3_ = bf16[1408,256]{1,0:T(8,128)(2,1)S(1)} collective-permute-done((bf16[1408,256]{1,0:T(8,128)(2,1)S(1)}, bf16[1408,256]{1,0:T(8,128)(2,1)S(1)}, u32[]{:S(2)}, u32[]{:S(2)}) %collective-permute-start.18) | collective-permute-done | bytes 720928 | tf_op jit(solution)/shard_map/ppermute | solution.py:487
  289.1 8.5 %collective-permute-done.20 = bf16[1024,256]{1,0:T(8,128)(2,1)S(1)} collective-permute-done((bf16[1024,256]{1,0:T(8,128)(2,1)}, bf16[1024,256]{1,0:T(8,128)(2,1)S(1)}, u32[]{:S(2)}, u32[]{:S(2)}) %collective-permute-start.20) | collective-permute-done | bytes 524320 | tf_op jit(solution)/shard_map/ppermute | solution.py:481
  302.5 10.5 %collective-permute-done.21 = f32[4864]{0:T(1024)S(1)} collective-permute-done((f32[4864]{0:T(1024)S(1)}, f32[4864]{0:T(1024)S(1)}, u32[]{:S(2)}, u32[]{:S(2)}) %collective-permute-start.21) | collective-permute-done | bytes 19488 | tf_op jit(solution)/shard_map/ppermute | solution.py:510
  314.2 28.9 %collective-permute-done.22 = f32[4864]{0:T(1024)S(1)} collective-permute-done((f32[4864]{0:T(1024)S(1)}, f32[4864]{0:T(1024)S(1)}, u32[]{:S(2)}, u32[]{:S(2)}) %collective-permute-start.22) | collective-permute-done | bytes 19488 | tf_op jit(solution)/shard_map/ppermute | solution.py:510
  347.9 3.2 fusion.11
  353.4 7.6 %place.4 = (f32[704,2048]{1,0:T(8,128)}, f32[704,2048]{1,0:T(8,128)}) custom-call(s32[8]{0:T(128)S(1)} %copy-done.15, bf16[1408,256]{1,0:T(8,128)(2,1)S(1)} %copy-done.2, bf16[1408,256]{1,0:T(8,128)(2,1)S(1)} %copy-done.3, bf16[1408,256]{1,0:T(8,128)(2,1)S(1)} %collective-permute-done.17.refs_2_, bf16[1408,256]{1,0:T(8,128)(2,1)S(1)} %copy-done.5, ...), custom_call_target="tpu_custom_call" | custom-call | flops 6499999744 | tf_op jit(solution)/shard_map/place/pallas_call | solution.py:408
  361.0 7.0 %collective-permute-done.28.refs_5_ = bf16[2048,256]{1,0:T(8,128)(2,1)} collective-permute-done((bf16[2048,256]{1,0:T(8,128)(2,1)}, bf16[2048,256]{1,0:T(8,128)(2,1)}, u32[]{:S(2)}, u32[]{:S(2)}) %collective-permute-start.28) | collective-permute-done | bytes 1048608 | tf_op jit(solution)/shard_map/ppermute | solution.py:493
  369.4 6.6 %place.5 = (f32[768,2048]{1,0:T(8,128)}, f32[256,2048]{1,0:T(8,128)}) custom-call(s32[8]{0:T(128)S(1)} %copy-done.15, bf16[1024,256]{1,0:T(8,128)(2,1)S(1)} %add.203.refs_0_, bf16[1024,256]{1,0:T(8,128)(2,1)S(1)} %add.204.refs_1_, bf16[1024,256]{1,0:T(8,128)(2,1)S(1)} %copy-done.13, bf16[1024,256]{1,0:T(8,128)(2,1)S(1)} %copy-done.11, ...), custom_call_target="tpu_custom_call" | custom-call | flops 6499999744 | tf_op jit(solution)/shard_map/place/pallas_call | solution.py:408
  (247 shorter events, 63.0 us)
Async XLA Ops:
  7.2 56.3 %all-gather.3.cloned.1.call-start = ((), (), s32[]{:S(2)}) async-start(), calls=%async_computation.2 | async-start | bytes 4718592 | tf_op jit(solution)/shard_map/all_gather | solution.py:554
  11.3 52.4 %copy-start.71 = (bf16[3,256]{1,0:T(4,128)(2,1)S(1)}, bf16[3,256]{1,0:T(4,128)(2,1)}, u32[]{:S(2)}) copy-start(bf16[3,256]{1,0:T(4,128)(2,1)} %param.15) | copy-start | bytes 4612
  13.5 98.1 %all-gather.5.cloned.1.call-start = ((), (), s32[]{:S(2)}) async-start(), calls=%async_computation.4 | async-start | bytes 4718592 | tf_op jit(solution)/shard_map/all_gather | solution.py:556
  14.0 52.2 %copy-start.69 = (pred[128]{0:T(512)(128)(4,1)}, pred[128]{0:T(512)(128)(4,1)S(1)}, u32[]{:S(2)}) copy-start(pred[128]{0:T(512)(128)(4,1)S(1)} %dynamic_slice.3) | copy-start | bytes 388
  63.6 196.9 %reduce-scatter.5.cloned.1.call-start = ((), (), s32[]{:S(2)}) async-start(), calls=%async_computation.5 | async-start | bytes 4718592 | tf_op jit(solution)/shard_map/reduce_scatter | solution.py:599
  80.7 12.7 %copy-start.26 = (bf16[704,2048]{1,0:T(8,128)(2,1)S(1)}, bf16[704,2048]{1,0:T(8,128)(2,1)}, u32[]{:S(2)}) copy-start(bf16[704,2048]{1,0:T(8,128)(2,1)} %down_weight.1) | copy-start | bytes 8650756
  80.7 12.7 %copy-start.32 = (bf16[256,2048]{1,0:T(8,128)(2,1)S(1)}, bf16[256,2048]{1,0:T(8,128)(2,1)}, u32[]{:S(2)}) copy-start(bf16[256,2048]{1,0:T(8,128)(2,1)} %out_weight.1) | copy-start | bytes 3145732
  117.4 20.5 %collective-permute-start = (bf16[704,512]{1,0:T(8,128)(2,1)S(1)}, bf16[704,512]{1,0:T(8,128)(2,1)S(1)}, u32[]{:S(2)}, u32[]{:S(2)}) collective-permute-start(bf16[704,512]{1,0:T(8,128)(2,1)S(1)} %get-tuple-element.84), channel_id=1, source_target_pairs={{0,8},{8,0},{16,24},{24,16},{1,9},{9,1},{17,25},{25,17},{2,10},{10... | collective-permute-start | bytes 2162696 | tf_op jit(solution)/shard_map/ppermute | solution.py:463
  118.9 19.0 %collective-permute-start.1 = (bf16[704,512]{1,0:T(8,128)(2,1)S(1)}, bf16[704,512]{1,0:T(8,128)(2,1)S(1)}, u32[]{:S(2)}, u32[]{:S(2)}) collective-permute-start(bf16[704,512]{1,0:T(8,128)(2,1)S(1)} %get-tuple-element.97), channel_id=1, source_target_pairs={{0,16},{16,0},{8,24},{24,8},{1,17},{17,1},{9,25},{25,9},{2,18},{18... | collective-permute-start | bytes 2162696 | tf_op jit(solution)/shard_map/ppermute | solution.py:463
  132.8 48.3 %collective-permute-start.4 = (bf16[1408,512]{1,0:T(8,128)(2,1)}, bf16[1408,512]{1,0:T(8,128)(2,1)}, u32[]{:S(2)}, u32[]{:S(2)}) collective-permute-start(bf16[1408,512]{1,0:T(8,128)(2,1)} %get-tuple-element.95), channel_id=1, source_target_pairs={{0,8},{8,0},{16,24},{24,16},{1,9},{9,1},{17,25},{25,17},{2,10},{10... | collective-permute-start | bytes 4325384 | tf_op jit(solution)/shard_map/ppermute | solution.py:463
  133.3 47.7 %collective-permute-start.5 = (bf16[1408,512]{1,0:T(8,128)(2,1)}, bf16[1408,512]{1,0:T(8,128)(2,1)}, u32[]{:S(2)}, u32[]{:S(2)}) collective-permute-start(bf16[1408,512]{1,0:T(8,128)(2,1)} %get-tuple-element.109), channel_id=1, source_target_pairs={{0,16},{16,0},{8,24},{24,8},{1,17},{17,1},{9,25},{25,9},{2,18},{18... | collective-permute-start | bytes 4325384 | tf_op jit(solution)/shard_map/ppermute | solution.py:463
  141.0 36.7 %collective-permute-start.2 = (bf16[704,256]{1,0:T(8,128)(2,1)S(1)}, bf16[704,256]{1,0:T(8,128)(2,1)}, u32[]{:S(2)}, u32[]{:S(2)}) collective-permute-start(bf16[704,256]{1,0:T(8,128)(2,1)S(1)} %get-tuple-element.98), channel_id=1, source_target_pairs={{0,16},{16,0},{8,24},{24,8},{1,17},{17,1},{9,25},{25,9},{2,18},{18... | collective-permute-start | bytes 1081352 | tf_op jit(solution)/shard_map/ppermute | solution.py:481
  142.5 32.0 %collective-permute-start.3 = (bf16[704,256]{1,0:T(8,128)(2,1)}, bf16[704,256]{1,0:T(8,128)(2,1)}, u32[]{:S(2)}, u32[]{:S(2)}) collective-permute-start(bf16[704,256]{1,0:T(8,128)(2,1)} %get-tuple-element.107), channel_id=1, source_target_pairs={{0,8},{8,0},{16,24},{24,16},{1,9},{9,1},{17,25},{25,17},{2,10},{10... | collective-permute-start | bytes 1081352 | tf_op jit(solution)/shard_map/ppermute | solution.py:481
  143.0 14.4 %copy-start.25 = (bf16[3,256,2048]{2,1,0:T(8,128)(2,1)S(1)}, bf16[3,256,2048]{2,1,0:T(8,128)(2,1)}, u32[]{:S(2)}) copy-start(bf16[3,256,2048]{2,1,0:T(8,128)(2,1)} %param.14) | copy-start | bytes 9437188
  143.0 14.4 %copy-start.29 = (bf16[704,2048]{1,0:T(8,128)(2,1)S(1)}, bf16[704,2048]{1,0:T(8,128)(2,1)}, u32[]{:S(2)}) copy-start(bf16[704,2048]{1,0:T(8,128)(2,1)} %refs_3_.3) | copy-start | bytes 8650756
  143.0 14.4 %copy-start.31 = (bf16[704,2048]{1,0:T(8,128)(2,1)S(1)}, bf16[704,2048]{1,0:T(8,128)(2,1)}, u32[]{:S(2)}) copy-start(bf16[704,2048]{1,0:T(8,128)(2,1)} %refs_4_.1) | copy-start | bytes 8650756
  169.9 178.0 %reduce-scatter.3.cloned.1.call-start = ((), (), s32[]{:S(2)}) async-start(), calls=%async_computation.3 | async-start | bytes 4718592 | tf_op jit(solution)/shard_map/reduce_scatter | solution.py:608
  176.3 15.6 %collective-permute-start.7 = (bf16[704,256]{1,0:T(8,128)(2,1)}, bf16[704,256]{1,0:T(8,128)(2,1)}, u32[]{:S(2)}, u32[]{:S(2)}) collective-permute-start(bf16[704,256]{1,0:T(8,128)(2,1)} %add.186.refs_1_), channel_id=1, source_target_pairs={{0,8},{8,0},{16,24},{24,16},{1,9},{9,1},{17,25},{25,17},{2,10},{10... | collective-permute-start | bytes 1081352 | tf_op jit(solution)/shard_map/ppermute | solution.py:487
  179.6 15.8 %collective-permute-start.6 = (bf16[704,256]{1,0:T(8,128)(2,1)}, bf16[704,256]{1,0:T(8,128)(2,1)}, u32[]{:S(2)}, u32[]{:S(2)}) collective-permute-start(bf16[704,256]{1,0:T(8,128)(2,1)} %add.185.refs_0_), channel_id=1, source_target_pairs={{0,16},{16,0},{8,24},{24,8},{1,17},{17,1},{9,25},{25,9},{2,18},{18... | collective-permute-start | bytes 1081352 | tf_op jit(solution)/shard_map/ppermute | solution.py:487
  192.9 19.1 %collective-permute-start.9 = (bf16[1408,256]{1,0:T(8,128)(2,1)S(1)}, bf16[1408,256]{1,0:T(8,128)(2,1)S(1)}, u32[]{:S(2)}, u32[]{:S(2)}) collective-permute-start(bf16[1408,256]{1,0:T(8,128)(2,1)S(1)} %constant_dynamic-update-slice_fusion.2), channel_id=1, source_target_pairs={{0,16},{16,0},{8,24},{24,8},{1,17},{17,1},{9,25},{25,9},{2,18},{18... | collective-permute-start | bytes 2162696 | tf_op jit(solution)/shard_map/ppermute | solution.py:493
  197.1 19.4 %collective-permute-start.8 = (bf16[1408,256]{1,0:T(8,128)(2,1)}, bf16[1408,256]{1,0:T(8,128)(2,1)}, u32[]{:S(2)}, u32[]{:S(2)}) collective-permute-start(bf16[1408,256]{1,0:T(8,128)(2,1)} %constant_dynamic-update-slice_fusion), channel_id=1, source_target_pairs={{0,8},{8,0},{16,24},{24,16},{1,9},{9,1},{17,25},{25,17},{2,10},{10... | collective-permute-start | bytes 2162696 | tf_op jit(solution)/shard_map/ppermute | solution.py:493
  203.7 50.4 %collective-permute-start.13 = (bf16[1024,512]{1,0:T(8,128)(2,1)}, bf16[1024,512]{1,0:T(8,128)(2,1)S(1)}, u32[]{:S(2)}, u32[]{:S(2)}) collective-permute-start(bf16[1024,512]{1,0:T(8,128)(2,1)} %get-tuple-element.124), channel_id=1, source_target_pairs={{0,16},{16,0},{8,24},{24,8},{1,17},{17,1},{9,25},{25,9},{2,18},{18... | collective-permute-start | bytes 3145736 | tf_op jit(solution)/shard_map/ppermute | solution.py:463
  205.2 49.0 %collective-permute-start.12 = (bf16[1024,512]{1,0:T(8,128)(2,1)}, bf16[1024,512]{1,0:T(8,128)(2,1)}, u32[]{:S(2)}, u32[]{:S(2)}) collective-permute-start(bf16[1024,512]{1,0:T(8,128)(2,1)} %get-tuple-element.117), channel_id=1, source_target_pairs={{0,8},{8,0},{16,24},{24,16},{1,9},{9,1},{17,25},{25,17},{2,10},{10... | collective-permute-start | bytes 3145736 | tf_op jit(solution)/shard_map/ppermute | solution.py:463
  206.7 41.2 %collective-permute-start.10 = (bf16[1408,256]{1,0:T(8,128)(2,1)}, bf16[1408,256]{1,0:T(8,128)(2,1)S(1)}, u32[]{:S(2)}, u32[]{:S(2)}) collective-permute-start(bf16[1408,256]{1,0:T(8,128)(2,1)} %get-tuple-element.112), channel_id=1, source_target_pairs={{0,16},{16,0},{8,24},{24,8},{1,17},{17,1},{9,25},{25,9},{2,18},{18... | collective-permute-start | bytes 2162696 | tf_op jit(solution)/shard_map/ppermute | solution.py:481
  213.0 39.0 %collective-permute-start.11 = (bf16[1408,256]{1,0:T(8,128)(2,1)}, bf16[1408,256]{1,0:T(8,128)(2,1)}, u32[]{:S(2)}, u32[]{:S(2)}) collective-permute-start(bf16[1408,256]{1,0:T(8,128)(2,1)} %get-tuple-element.122), channel_id=1, source_target_pairs={{0,8},{8,0},{16,24},{24,16},{1,9},{9,1},{17,25},{25,17},{2,10},{10... | collective-permute-start | bytes 2162696 | tf_op jit(solution)/shard_map/ppermute | solution.py:481
  217.6 36.6 %copy-start.23 = (bf16[1024,2048]{1,0:T(8,128)(2,1)S(1)}, bf16[1024,2048]{1,0:T(8,128)(2,1)}, u32[]{:S(2)}) copy-start(bf16[1024,2048]{1,0:T(8,128)(2,1)} %all-gather.5.cloned.1.call-done.refs_1_.grad_all.refs_3_) | copy-start | bytes 12582916
  217.6 36.6 %copy-start.42 = (bf16[768,1024]{1,0:T(8,128)(2,1)S(1)}, bf16[768,1024]{1,0:T(8,128)(2,1)}, u32[]{:S(2)}) copy-start(bf16[768,1024]{1,0:T(8,128)(2,1)} %copy-done.40) | copy-start | bytes 4718596
  217.6 36.6 %copy-start.53 = (bf16[256,1024]{1,0:T(8,128)(2,1)S(1)}, bf16[256,1024]{1,0:T(8,128)(2,1)}, u32[]{:S(2)}) copy-start(bf16[256,1024]{1,0:T(8,128)(2,1)} %copy-done.51) | copy-start | bytes 1572868
  254.3 14.6 %copy-start.3 = (bf16[1408,256]{1,0:T(8,128)(2,1)S(1)}, bf16[1408,256]{1,0:T(8,128)(2,1)}, u32[]{:S(2)}) copy-start(bf16[1408,256]{1,0:T(8,128)(2,1)} %add.198.refs_1_) | copy-start | bytes 2162692
  262.2 1.6 collective-permute-start.14
  262.3 19.0 %collective-permute-start.17 = (bf16[1408,256]{1,0:T(8,128)(2,1)S(1)}, bf16[1408,256]{1,0:T(8,128)(2,1)S(1)}, u32[]{:S(2)}, u32[]{:S(2)}) collective-permute-start(bf16[1408,256]{1,0:T(8,128)(2,1)S(1)} %copy-done.2), channel_id=1, source_target_pairs={{0,16},{16,0},{8,24},{24,8},{1,17},{17,1},{9,25},{25,9},{2,18},{18... | collective-permute-start | bytes 2162696 | tf_op jit(solution)/shard_map/ppermute | solution.py:487
  263.8 3.8 collective-permute-start.15
  267.7 4.6 %collective-permute-start.16 = (f32[4096]{0:T(1024)S(1)}, f32[4096]{0:T(1024)S(1)}, u32[]{:S(2)}, u32[]{:S(2)}) collective-permute-start(f32[4096]{0:T(1024)S(1)} %add.201), channel_id=1, source_target_pairs={{0,4},{1,5},{2,6},{3,7},{4,0},{5,1},{6,2},{7,3},{8,12},{9,13},{10,... | collective-permute-start | bytes 49160 | tf_op jit(solution)/shard_map/ppermute | solution.py:510
  268.8 19.1 %collective-permute-start.18 = (bf16[1408,256]{1,0:T(8,128)(2,1)S(1)}, bf16[1408,256]{1,0:T(8,128)(2,1)S(1)}, u32[]{:S(2)}, u32[]{:S(2)}) collective-permute-start(bf16[1408,256]{1,0:T(8,128)(2,1)S(1)} %copy-done.3), channel_id=1, source_target_pairs={{0,8},{8,0},{16,24},{24,16},{1,9},{9,1},{17,25},{25,17},{2,10},{10... | collective-permute-start | bytes 2162696 | tf_op jit(solution)/shard_map/ppermute | solution.py:487
  269.8 28.5 %collective-permute-start.19 = (bf16[1024,256]{1,0:T(8,128)(2,1)S(1)}, bf16[1024,256]{1,0:T(8,128)(2,1)S(1)}, u32[]{:S(2)}, u32[]{:S(2)}) collective-permute-start(bf16[1024,256]{1,0:T(8,128)(2,1)S(1)} %get-tuple-element.125), channel_id=1, source_target_pairs={{0,16},{16,0},{8,24},{24,8},{1,17},{17,1},{9,25},{25,9},{2,18},{18... | collective-permute-start | bytes 1572872 | tf_op jit(solution)/shard_map/ppermute | solution.py:481
  270.9 26.7 %collective-permute-start.20 = (bf16[1024,256]{1,0:T(8,128)(2,1)}, bf16[1024,256]{1,0:T(8,128)(2,1)S(1)}, u32[]{:S(2)}, u32[]{:S(2)}) collective-permute-start(bf16[1024,256]{1,0:T(8,128)(2,1)} %copy-done.36), channel_id=1, source_target_pairs={{0,8},{8,0},{16,24},{24,16},{1,9},{9,1},{17,25},{25,17},{2,10},{10... | collective-permute-start | bytes 1572872 | tf_op jit(solution)/shard_map/ppermute | solution.py:481
  274.1 23.4 %copy-start.9 = (bf16[1024,256]{1,0:T(8,128)(2,1)S(1)}, bf16[1024,256]{1,0:T(8,128)(2,1)}, u32[]{:S(2)}) copy-start(bf16[1024,256]{1,0:T(8,128)(2,1)} %copy-done.8) | copy-start | bytes 1572868
  282.2 16.1 %copy-start.7 = (bf16[1024,256]{1,0:T(8,128)(2,1)S(1)}, bf16[1024,256]{1,0:T(8,128)(2,1)}, u32[]{:S(2)}) copy-start(bf16[1024,256]{1,0:T(8,128)(2,1)} %copy-done.6) | copy-start | bytes 1572868
  297.7 47.0 %collective-permute-start.24 = (bf16[1024,256]{1,0:T(8,128)(2,1)S(1)}, bf16[1024,256]{1,0:T(8,128)(2,1)S(1)}, u32[]{:S(2)}, u32[]{:S(2)}) collective-permute-start(bf16[1024,256]{1,0:T(8,128)(2,1)S(1)} %add.204.refs_1_), channel_id=1, source_target_pairs={{0,8},{8,0},{16,24},{24,16},{1,9},{9,1},{17,25},{25,17},{2,10},{10... | collective-permute-start | bytes 1572872 | tf_op jit(solution)/shard_map/ppermute | solution.py:487
  298.4 14.6 %collective-permute-start.21 = (f32[4864]{0:T(1024)S(1)}, f32[4864]{0:T(1024)S(1)}, u32[]{:S(2)}, u32[]{:S(2)}) collective-permute-start(f32[4864]{0:T(1024)S(1)} %pad_maximum_fusion.1), channel_id=1, source_target_pairs={{0,8},{8,0},{16,24},{24,16},{1,9},{9,1},{17,25},{25,17},{2,10},{10... | collective-permute-start | bytes 58376 | tf_op jit(solution)/shard_map/ppermute | solution.py:510
  300.0 46.5 %collective-permute-start.23 = (bf16[1024,256]{1,0:T(8,128)(2,1)S(1)}, bf16[1024,256]{1,0:T(8,128)(2,1)S(1)}, u32[]{:S(2)}, u32[]{:S(2)}) collective-permute-start(bf16[1024,256]{1,0:T(8,128)(2,1)S(1)} %add.203.refs_0_), channel_id=1, source_target_pairs={{0,16},{16,0},{8,24},{24,8},{1,17},{17,1},{9,25},{25,9},{2,18},{18... | collective-permute-start | bytes 1572872 | tf_op jit(solution)/shard_map/ppermute | solution.py:487
  301.1 51.2 %collective-permute-start.26 = (bf16[2816,256]{1,0:T(8,128)(2,1)}, bf16[2816,256]{1,0:T(8,128)(2,1)}, u32[]{:S(2)}, u32[]{:S(2)}) collective-permute-start(bf16[2816,256]{1,0:T(8,128)(2,1)} %constant_dynamic-update-slice_fusion.6), channel_id=1, source_target_pairs={{0,16},{16,0},{8,24},{24,8},{1,17},{17,1},{9,25},{25,9},{2,18},{18... | collective-permute-start | bytes 4325384 | tf_op jit(solution)/shard_map/ppermute | solution.py:493
  302.0 50.3 %collective-permute-start.25 = (bf16[2816,256]{1,0:T(8,128)(2,1)}, bf16[2816,256]{1,0:T(8,128)(2,1)}, u32[]{:S(2)}, u32[]{:S(2)}) collective-permute-start(bf16[2816,256]{1,0:T(8,128)(2,1)} %constant_dynamic-update-slice_fusion.4), channel_id=1, source_target_pairs={{0,8},{8,0},{16,24},{24,16},{1,9},{9,1},{17,25},{25,17},{2,10},{10... | collective-permute-start | bytes 4325384 | tf_op jit(solution)/shard_map/ppermute | solution.py:493
  313.1 30.0 %collective-permute-start.22 = (f32[4864]{0:T(1024)S(1)}, f32[4864]{0:T(1024)S(1)}, u32[]{:S(2)}, u32[]{:S(2)}) collective-permute-start(f32[4864]{0:T(1024)S(1)} %add.205), channel_id=1, source_target_pairs={{0,16},{8,24},{16,0},{24,8},{1,17},{9,25},{17,1},{25,9},{2,18},{10... | collective-permute-start | bytes 58376 | tf_op jit(solution)/shard_map/ppermute | solution.py:510
  345.6 22.4 %collective-permute-start.28 = (bf16[2048,256]{1,0:T(8,128)(2,1)}, bf16[2048,256]{1,0:T(8,128)(2,1)}, u32[]{:S(2)}, u32[]{:S(2)}) collective-permute-start(bf16[2048,256]{1,0:T(8,128)(2,1)} %constant_dynamic-update-slice_fusion.10), channel_id=1, source_target_pairs={{0,16},{16,0},{8,24},{24,8},{1,17},{17,1},{9,25},{25,9},{2,18},{18... | collective-permute-start | bytes 3145736 | tf_op jit(solution)/shard_map/ppermute | solution.py:493
  347.5 21.9 %collective-permute-start.27 = (bf16[2048,256]{1,0:T(8,128)(2,1)}, bf16[2048,256]{1,0:T(8,128)(2,1)}, u32[]{:S(2)}, u32[]{:S(2)}) collective-permute-start(bf16[2048,256]{1,0:T(8,128)(2,1)} %constant_dynamic-update-slice_fusion.8), channel_id=1, source_target_pairs={{0,8},{8,0},{16,24},{24,16},{1,9},{9,1},{17,25},{25,17},{2,10},{10... | collective-permute-start | bytes 3145736 | tf_op jit(solution)/shard_map/ppermute | solution.py:493
  353.4 16.0 %copy-start.11 = (bf16[1024,256]{1,0:T(8,128)(2,1)S(1)}, bf16[1024,256]{1,0:T(8,128)(2,1)}, u32[]{:S(2)}) copy-start(bf16[1024,256]{1,0:T(8,128)(2,1)} %copy-done.10) | copy-start | bytes 1572868
  353.4 16.0 %copy-start.13 = (bf16[1024,256]{1,0:T(8,128)(2,1)S(1)}, bf16[1024,256]{1,0:T(8,128)(2,1)}, u32[]{:S(2)}) copy-start(bf16[1024,256]{1,0:T(8,128)(2,1)} %copy-done.12) | copy-start | bytes 1572868
  (58 other events, 213.0 us)
Sparse Core Ops, SparseCore 0:
  13.7 49.8 all-gather.2
  65.7 45.8 all-gather.4
  170.0 47.8 reduce-scatter.4
  220.6 48.3 reduce-scatter.2
